TPU v7x, 32 devices: a whole 2x2x4 slice. The times are simulated.
32 devices in a mesh: grp: 2 (over y), side: 4 (over z), shard: 4 (over x, core).
Axes of the slice: x: 2, y: 2, z: 4, core: 2. Of those that a mesh axis runs over, the one named last changes fastest.
Arguments:
- queries: bfloat16 [480, 8192], P(('grp', 'side', 'shard')), parts along dimension 0, may hold values from -6.5 to 6.5
- new_kv: bfloat16 [480, 2048], P(('grp', 'side', 'shard')), parts along dimension 0, may hold values from -4.5 to 4.5
- kv_pool: bfloat16 [3584, 16, 2048], P(('grp', 'side', 'shard')), parts along dimension 0, may hold values from -4.5 to 4.5
- page_table: int32 [480, 16], P(('grp', 'side', 'shard')), parts along dimension 0, may hold values from 0 to 111, as said below
- ctx_len: int32 [480], P(('grp', 'side', 'shard')), parts along dimension 0, may hold values from 0 to 256, as said below
- residual_in: bfloat16 [480, 8192], P(('grp', 'side', 'shard')), parts along dimension 0, may hold values from -6 to 6
- norm_gain: bfloat16 [8192], replicated, may hold values from 0.5 to 1.5
- w_up: bfloat16 [8192, 16384], P('side', 'shard'), may hold values from -0.0625 to 0.0625
- w_down: bfloat16 [16384, 8192], P('shard', 'side'), may hold values from -0.046875 to 0.046875
Outputs:
- layer_out: bfloat16 [480, 8192], P(('grp', 'side', 'shard')), parts along dimension 0
There are 2 independent parts, one for each index of `grp`. A program takes and returns all parts, laid end to end along the dimension named above; an argument that names none is the same for every part. Nothing has to cross between parts.
Inputs may be any that keep to these rules, and one draw needn't show every extreme that they name: `ctx_len`: on one device's 15 slots, 3 to 12 have a nonzero length, exactly 12 on some device; a live slot's pages together hold at most 112 pages on its device; every device has a slot of length 256. `page_table`: the first ceil(ctx_len / 16) entries of a live slot name distinct pages, and no page is named by two live slots of one device; other entries name valid pages.
All inputs are finite; a program needn't handle non-finite values.
Results may differ from a plain program's by a relative error of at most 0.009.
Values may be sent and summed in bfloat16 or wider, within the bound.
No kernel may reach another device: no remote copies, remote signals or barrier semaphores. Data moves between devices by JAX's collectives and lax.ppermute only.
A program may use at most 128 MiB of HBM per device.

v0:
```python
import functools
import math

import jax
import jax.numpy as jnp
from jax import lax
from jax.experimental import pallas as pl
from jax.experimental.pallas import tpu as pltpu
from jax.sharding import PartitionSpec as P

KV_HEADS = 8
HEAD = 128
GROUP = 8
LIVE_CAP = 12
PAD = 16
TALL = 2 * LIVE_CAP
EMPTY = 1e30

epsilon = 1e-05
bf16, f32, i32 = jnp.bfloat16, jnp.float32, jnp.int32
VMEM_MB = 1 << 20


def params(mb, **more):
    return pltpu.CompilerParams(vmem_limit_bytes=mb * VMEM_MB, **more)


def cost(flops, bytes_accessed):
    return pl.CostEstimate(
        flops=int(flops) // 64, bytes_accessed=int(bytes_accessed) // 64, transcendentals=0
    )


def pad_rows(x):
    rows = x.shape[0]
    if rows == PAD:
        return x
    return jnp.concatenate([x, jnp.zeros((PAD - rows,) + x.shape[1:], x.dtype)], axis=0)


def live_ranks(lengths, slots):
    live, rank, count = [], [], jnp.int32(0)
    for slot in range(slots):
        alive = lengths[slot] > 0
        live.append(alive)
        rank.append(count)
        count = count + alive.astype(i32)
    return live, rank


def token_bias(lengths, table, pages, page):
    slots, entries = table.shape
    tokens = pages * page
    lanes = 128 * ((pages + 127) // 128)
    row = lax.broadcasted_iota(i32, (PAD, lanes), 0)
    column = lax.broadcasted_iota(i32, (PAD, lanes), 1)
    reach = jnp.zeros((PAD, lanes), i32)
    for slot in range(slots):
        reach = jnp.where(row == slot, lengths[slot], reach)
    table = pad_rows(table)
    seen = jnp.zeros((PAD, lanes), i32)
    for entry in range(entries):
        here = jnp.minimum(jnp.maximum(reach - entry * page, 0), page)
        seen = seen + jnp.where(table[:, entry : entry + 1] == column, here, 0)
    spread = (
        lax.broadcasted_iota(i32, (lanes, tokens), 1) // page
        == lax.broadcasted_iota(i32, (lanes, tokens), 0)
    )
    seen_tokens = jnp.dot(
        seen.astype(f32).astype(bf16), spread.astype(f32).astype(bf16), preferred_element_type=f32
    )
    place = (lax.broadcasted_iota(i32, (PAD, tokens), 1) % page).astype(f32)
    return jnp.where(place < seen_tokens, 0.0, -1e30)


def live_pick(lengths, of_rank, of_slot, slots):
    live, rank = live_ranks(lengths, slots)
    pick = jnp.zeros(of_rank.shape, f32)
    for slot in range(slots):
        chosen = jnp.logical_and(of_rank == rank[slot], of_slot == slot)
        pick = jnp.where(jnp.logical_and(chosen, live[slot]), 1.0, pick)
    return pick.astype(bf16), rank[-1] + live[-1].astype(i32)


def back_rank(row, t, tiles):
    first, last = row - 8 * t, row - 8 * tiles - (LIVE_CAP - 8) * t
    rest = jnp.where(jnp.logical_and(last >= 0, last < LIVE_CAP - 8), last + 8, -1)
    return jnp.where(jnp.logical_and(first >= 0, first < 8), first, rest)


POOL_CUTS = 4


def attend_kernel(*refs, masks, sides, first):
    side = lax.axis_index("side")
    refs = list(refs)
    take = lambda n: [refs.pop(0) for _ in range(n)]
    if first:
        lengths, table_ref = take(2)
        sources = take(4)
    else:
        q_ref, new_ref, res_ref, gain_ref, bias_ref, picks_ref, empty_ref = take(7)
    pool_source = refs.pop(0)
    sends, mixed_refs = take(len(masks)), take(len(masks))
    square_ref = refs.pop(0)
    if first:
        q_ref, new_ref, res_ref, gain_ref, bias_ref, picks_ref, empty_ref, back_ref = take(8)
        gain_copy, sems = take(2)
    pool_ref, pool_sems = refs
    slots, step = mixed_refs[0].shape
    pages, page, width = pool_source.shape
    columns = width // 2 // sides
    heads = columns // HEAD
    tokens = pages * page
    scale = math.log2(math.e) / math.sqrt(HEAD)

    if first:
        small = [
            pltpu.make_async_copy(source, target, sems.at[n])
            for n, (source, target) in enumerate(
                zip(sources, (q_ref, new_ref, res_ref, gain_copy), strict=True)
            )
        ]
        for copy in small:
            copy.start()
    cut, half, pair = pages // POOL_CUTS, width // 2, columns * 2
    here = lax.div(side ^ masks[0], 2) * pair
    brought = []
    for n, at in enumerate((here, half + here)):
        columns_at = pl.ds(pl.multiple_of(at, pair), pair)
        target_at = pl.ds(n * pair, pair)
        brought.append([])
        for c in range(POOL_CUTS):
            rows = pl.ds(c * cut, cut)
            copy = pltpu.make_async_copy(
                pool_source.at[rows, :, columns_at], pool_ref.at[rows, :, target_at], pool_sems.at[n, c]
            )
            copy.start()
            brought[n].append(copy)
    if first:
        bias_ref[...] = token_bias(lengths, table_ref[...], pages, page)
        rank, slot = (lax.broadcasted_iota(i32, (TALL, PAD), n) for n in range(2))
        for head in range(heads):
            picks_ref[head], count = live_pick(lengths, rank - head * LIVE_CAP, slot, slots)
        rank = lax.broadcasted_iota(i32, empty_ref.shape, 0)
        rank = jnp.where(rank < LIVE_CAP, rank, rank - LIVE_CAP)
        empty_ref[...] = (rank >= count).astype(f32)
        slot, row = (lax.broadcasted_iota(i32, back_ref.shape[1:], n) for n in range(2))
        for t in range(back_ref.shape[0]):
            rank = back_rank(row, t, back_ref.shape[0])
            back_ref[t] = live_pick(lengths, rank, slot, slots)[0]
        for copy in small:
            copy.wait()
        gain_ref[...] = gain_copy[...].astype(f32)
    for copy in brought[0]:
        copy.wait()
    values_to_come = brought[1]

    squares = jnp.zeros((slots, HEAD), f32)
    bias = bias_ref[...][None]
    jobs = [(n, head) for n in range(len(masks)) for head in range(heads)]

    def places(job):
        block, base = side ^ masks[job[0]], job[1] * GROUP * HEAD
        new_at = pl.multiple_of(block * columns, columns) + job[1] * HEAD
        key_at = pl.multiple_of(lax.rem(block, 2) * columns, columns) + job[1] * HEAD
        return block, base, pl.multiple_of(block * step, step) + base, new_at, key_at

    def score(job):
        _, _, start, new_at, key_at = places(job)
        q = jnp.concatenate(
            [pad_rows(q_ref[:, pl.ds(start + g * HEAD, HEAD)]) for g in range(GROUP)], axis=0
        )
        keys = pool_ref[:, :, pl.ds(key_at, HEAD)].reshape(tokens, HEAD)
        new_key = pad_rows(new_ref[:, pl.ds(new_at, HEAD)]).astype(f32)
        scores = lax.dot_general(q, keys, (((1,), (1,)), ((), ())), preferred_element_type=f32)
        own = jnp.sum(
            q.astype(f32).reshape(GROUP, PAD, HEAD) * new_key[None], axis=-1, keepdims=True
        )
        return scores.reshape(GROUP, PAD, tokens), own * scale

    ready = score(jobs[0])
    for number, job in enumerate(jobs):
        block, base, start, new_at, key_at = places(job)
        scores, own = ready
        if number + 1 < len(jobs):
            ready = score(jobs[number + 1])
        scores = scores * scale + bias
        highest = jnp.maximum(jnp.max(scores, axis=-1, keepdims=True), own)
        weights = jnp.exp2(scores - highest)
        own_weight = jnp.exp2(own - highest)
        total = jnp.sum(weights, axis=-1, keepdims=True) + own_weight
        for copy in values_to_come:
            copy.wait()
        values_to_come = []
        values = pool_ref[:, :, pl.ds(pair + key_at, HEAD)].reshape(tokens, HEAD)
        new_value = pad_rows(new_ref[:, pl.ds(half + new_at, HEAD)]).astype(f32)
        summed = jnp.dot(
            weights.astype(bf16).reshape(GROUP * PAD, tokens), values, preferred_element_type=f32
        ).reshape(GROUP, PAD, HEAD)
        attended = (summed + own_weight * new_value[None]) / total
        for g in range(GROUP):
            at = slice(base + g * HEAD, base + (g + 1) * HEAD)
            residual = res_ref[:, pl.ds(start + g * HEAD, HEAD)].astype(f32)
            mixed = residual + attended[g][:slots]
            mixed_refs[job[0]][:, at] = mixed
            squares = squares + mixed * mixed
            gain = gain_ref[pl.ds(block * (step // HEAD) + job[1] * GROUP + g, 1), :]
            gained = pad_rows((mixed * gain).astype(bf16))
            rows = jnp.dot(picks_ref[job[1]], gained, preferred_element_type=f32)
            to = slice(g * HEAD, (g + 1) * HEAD)
            if job[1]:
                rows = rows + sends[job[0]][:, to].astype(f32)
                rows = jnp.where(empty_ref[...] > 0, EMPTY, rows)
            sends[job[0]][:, to] = rows.astype(bf16)
    square_ref[...] = squares


def attend(inputs, sides, masks, before):
    queries, new_kv, kv_pool, page_table, ctx_len, residual_in, norm_gain = inputs
    slots, columns = queries.shape
    pages, page, _ = kv_pool.shape
    step = columns // sides
    first = before is None
    vmem, anywhere = pl.BlockSpec(memory_space=pltpu.VMEM), pl.BlockSpec(memory_space=pl.ANY)
    smem = pl.BlockSpec(memory_space=pltpu.SMEM)
    out_shape = [jax.ShapeDtypeStruct((TALL, step // 2), bf16)] * len(masks)
    out_shape += [jax.ShapeDtypeStruct((slots, step), f32)] * len(masks)
    out_shape += [jax.ShapeDtypeStruct((slots, HEAD), f32)]
    if first:
        operands = [ctx_len, page_table, queries, new_kv, residual_in, norm_gain, kv_pool]
        in_specs = [smem, vmem] + [anywhere] * 5
        tiles = step // DOWN_TILE
        out_shape += [
            pltpu.VMEM(queries.shape, bf16),
            pltpu.VMEM(new_kv.shape, bf16),
            pltpu.VMEM(residual_in.shape, bf16),
            pltpu.VMEM(norm_gain.shape, f32),
            pltpu.VMEM((PAD, pages * page), f32),
            pltpu.VMEM((columns // HEAD // GROUP // sides, TALL, PAD), bf16),
            pltpu.VMEM((TALL, HEAD), f32),
            pltpu.VMEM((tiles, PAD, tiles * LIVE_CAP), bf16),
        ]
        scratch = [pltpu.VMEM(norm_gain.shape, bf16), pltpu.SemaphoreType.DMA((4,))]
    else:
        operands = [*before, kv_pool]
        in_specs = [vmem] * len(before) + [anywhere]
        scratch = []
    scratch += [
        pltpu.VMEM((pages, page, kv_pool.shape[2] // sides * 2), bf16),
        pltpu.SemaphoreType.DMA((2, POOL_CUTS)),
    ]
    outs = pl.pallas_call(
        functools.partial(attend_kernel, masks=masks, sides=sides, first=first),
        in_specs=in_specs,
        out_specs=[vmem] * len(out_shape),
        out_shape=out_shape,
        scratch_shapes=scratch,
        compiler_params=params(28),
        cost_estimate=cost(2e9, kv_pool.size),
        name="attend",
    )(*operands)
    n = len(masks)
    return outs[:n], outs[n : 2 * n], outs[2 * n], outs[2 * n + 1 :]


UP_TILE = 256
DOWN_TILE = 512


def tile_copy(w_ref, row, rows, column, buffer, sems, t, tile):
    at = pl.ds(pl.multiple_of(t * tile, tile), tile)
    source = w_ref.at[pl.ds(row, rows), pl.ds(pl.multiple_of(column + t * tile, tile), tile)]
    return pltpu.make_async_copy(source, buffer.at[:, at], sems.at[t])


def up_kernel(x_ref, w_ref, *refs, masks, ahead):
    if ahead is None:
        out_ref, buffer, sems = refs
    else:
        down_ref, out_ref, next_ref, buffer, sems, next_sems = refs
    side = lax.axis_index("side")
    depth, width = buffer.shape[1:]
    tiles = width // UP_TILE

    def copy_of(n, t):
        column = pl.multiple_of(((side ^ masks[n][0]) * 2 + masks[n][1]) * width, width)
        return tile_copy(w_ref, 0, depth, column, buffer.at[n], sems.at[n], t, UP_TILE)

    for n in range(len(masks)):
        for t in range(tiles):
            copy_of(n, t).start()
    if ahead is not None:
        row = pl.multiple_of((side ^ ahead) * next_ref.shape[0], next_ref.shape[0])
        later = [
            tile_copy(down_ref, row, next_ref.shape[0], 0, next_ref, next_sems, t, DOWN_TILE)
            for t in range(next_ref.shape[1] // DOWN_TILE)
        ]
        for copy in later:
            copy.start()

    @pl.loop(0, len(masks) * tiles)
    def _(job):
        n, t = lax.div(job, tiles), lax.rem(job, tiles)
        at = pl.ds(pl.multiple_of(t * UP_TILE, UP_TILE), UP_TILE)
        pltpu.make_async_copy(
            w_ref.at[:, pl.ds(0, UP_TILE)], buffer.at[n, :, at], sems.at[n, t]
        ).wait()
        out_ref[n, :, at] = jnp.dot(
            x_ref[: out_ref.shape[1], :], buffer[n, :, at], preferred_element_type=f32
        ).astype(out_ref.dtype)

    if ahead is not None:
        for copy in later:
            copy.wait()


def up(packed, w_up, rows, width, masks, w_down=None, ahead=None):
    depth = w_up.shape[0]
    vmem, anywhere = pl.BlockSpec(memory_space=pltpu.VMEM), pl.BlockSpec(memory_space=pl.ANY)
    out = jax.ShapeDtypeStruct((len(masks), rows, width), bf16)
    scratch = [
        pltpu.VMEM((len(masks), depth, width), bf16),
        pltpu.SemaphoreType.DMA((len(masks), width // UP_TILE)),
    ]
    extra = ahead is not None
    if extra:
        out = [out, pltpu.VMEM((2 * width, w_down.shape[1]), bf16)]
        scratch.append(pltpu.SemaphoreType.DMA((w_down.shape[1] // DOWN_TILE,)))
    return pl.pallas_call(
        functools.partial(up_kernel, masks=masks, ahead=ahead),
        in_specs=[vmem, anywhere] + [anywhere] * extra,
        out_specs=[vmem, vmem] if extra else vmem,
        out_shape=out,
        scratch_shapes=scratch,
        compiler_params=params(24),
        cost_estimate=cost(2 * rows * depth * width, depth * width * 2 * len(masks)),
        name="up",
    )(packed, w_up, *([w_down] if extra else []))


PIECES = ((0, 2), (1, 3))


def find_layout(gathered, layout, step_ref, limits):
    side, shard = lax.axis_index("side"), lax.axis_index("shard")
    pieces = gathered[0].shape[0] // TALL
    devices = len(gathered) * pieces
    counts, places = [None] * devices, [None] * devices
    number = lax.broadcasted_iota(i32, (LIVE_CAP, HEAD), 0) + 1
    for part in range(len(gathered)):
        marks = gathered[part][:, :HEAD].astype(f32)
        for piece, mask in enumerate(PIECES[part % 2]):
            rows = marks[piece * TALL : piece * TALL + LIVE_CAP]
            last = jnp.where(rows < EMPTY / 2, number, 0).astype(f32)
            place = part // 2 * 4 + mask
            counts[place] = jnp.max(last).astype(i32)
            places[place] = (side ^ mask) * 4 + (shard ^ (part // 2))
    total = jnp.int32(0)
    for one in range(devices):
        base = jnp.int32(0)
        for other in range(devices):
            base = base + jnp.where(places[other] < places[one], counts[other], 0)
        layout[one] = base
        layout[devices + one] = counts[one]
        total = total + counts[one]
    step = jnp.int32(0)
    for limit in limits:
        step = step + (total > limit).astype(i32)
    step_ref[0] = step


def pack_up_kernel(*refs, mask, limits):
    gathered, refs = refs[:-7], refs[-7:]
    w_ref, packed_ref, out_ref, layout, step_ref, buffer, sems = refs
    width = out_ref.shape[1]

    def copy_of(t):
        column = pl.multiple_of((lax.axis_index("side") ^ mask) * 2 * width, width)
        return tile_copy(w_ref, 0, buffer.shape[0], column, buffer, sems, t, UP_TILE)

    for t in range(width // UP_TILE):
        copy_of(t).start()
    find_layout(gathered, layout, step_ref, limits)
    rows, depth = packed_ref.shape
    per = gathered[0].shape[0]
    pieces = per // TALL
    devices = len(gathered) * pieces
    shape = (8, len(gathered) * per)
    lane = lax.broadcasted_iota(i32, shape, 1)
    row = lax.broadcasted_iota(i32, (rows, shape[1]), 0)
    for half in range(2):
        target = jnp.full(shape, -1, i32)
        for part in range(len(gathered)):
            for piece, other in enumerate(PIECES[part % 2]):
                place = part // 2 * 4 + other
                base, count = layout[place], layout[devices + place]
                inside = lane - (part * per + piece * TALL + half * LIVE_CAP)
                mine = jnp.logical_and(inside >= 0, inside < count)
                target = jnp.where(mine, base + inside, target)
        pick = (target[:1] == row).astype(f32).astype(bf16)

        @pl.loop(0, depth // 2 // DOWN_TILE)
        def _(t):
            at = pl.ds(pl.multiple_of(t * DOWN_TILE, DOWN_TILE), DOWN_TILE)
            to = pl.ds(pl.multiple_of(half * (depth // 2) + t * DOWN_TILE, DOWN_TILE), DOWN_TILE)
            found = jnp.concatenate([part[:, at] for part in gathered], axis=0)
            packed_ref[:, to] = jnp.dot(pick, found, preferred_element_type=f32).astype(bf16)

    @pl.loop(0, width // UP_TILE)
    def _(t):
        copy_of(t).wait()
        at = pl.ds(pl.multiple_of(t * UP_TILE, UP_TILE), UP_TILE)
        out_ref[:, at] = jnp.dot(
            packed_ref[...], buffer[:, at], preferred_element_type=f32
        ).astype(bf16)


def pack_up(gathered, w_up, rows, width, mask, limits):
    depth = w_up.shape[0]
    devices = len(gathered) * gathered[0].shape[0] // TALL
    vmem, smem = pl.BlockSpec(memory_space=pltpu.VMEM), pl.BlockSpec(memory_space=pltpu.SMEM)
    return pl.pallas_call(
        functools.partial(pack_up_kernel, mask=mask, limits=limits),
        in_specs=[vmem] * len(gathered) + [pl.BlockSpec(memory_space=pl.ANY)],
        out_specs=[vmem, vmem, smem, smem],
        out_shape=[
            jax.ShapeDtypeStruct((rows, depth), bf16),
            jax.ShapeDtypeStruct((rows, width), bf16),
            jax.ShapeDtypeStruct((2 * devices,), i32),
            jax.ShapeDtypeStruct((1,), i32),
        ],
        scratch_shapes=[
            pltpu.VMEM((depth, width), bf16),
            pltpu.SemaphoreType.DMA((width // UP_TILE,)),
        ],
        compiler_params=params(24),
        cost_estimate=cost(2 * rows * depth * width, depth * width * 2),
        name="pack_up",
    )(*gathered, w_up)


def down_kernel(*refs, first, mask, ahead):
    refs = list(refs)
    a_ref, w_ref = refs.pop(0), refs.pop(0)
    before_ref = None if first else refs.pop(0)
    out_ref = refs.pop(0)
    next_ref = refs.pop(0) if ahead is not None else None
    buffer, sems = refs.pop(0), refs.pop(0)
    depth, width = buffer.shape
    tiles = width // DOWN_TILE

    def copy_of(other, buffer, sems, t):
        row = pl.multiple_of((lax.axis_index("side") ^ other) * depth, depth)
        return tile_copy(w_ref, row, depth, 0, buffer, sems, t, DOWN_TILE)

    for t in range(tiles):
        copy_of(mask, buffer, sems, t).start()
    if ahead is not None:
        for t in range(tiles):
            copy_of(ahead, next_ref, refs[0], t).start()

    @pl.loop(0, tiles)
    def _(t):
        at = pl.ds(pl.multiple_of(t * DOWN_TILE, DOWN_TILE), DOWN_TILE)
        copy_of(mask, buffer, sems, t).wait()
        part = jnp.dot(a_ref[...], buffer[:, at], preferred_element_type=f32)
        out_ref[:, at] = part if first else before_ref[:, at] + part

    if ahead is not None:

        @pl.loop(0, tiles)
        def _(t):
            copy_of(ahead, next_ref, refs[0], t).wait()


def down(active, w_down, before, mask, ahead=None):
    rows, depth = active.shape
    width = w_down.shape[1]
    vmem = pl.BlockSpec(memory_space=pltpu.VMEM)
    out = jax.ShapeDtypeStruct((rows, width), f32)
    sems = pltpu.SemaphoreType.DMA((width // DOWN_TILE,))
    return pl.pallas_call(
        functools.partial(down_kernel, first=before is None, mask=mask, ahead=ahead),
        in_specs=[vmem, pl.BlockSpec(memory_space=pl.ANY)]
        + ([] if before is None else [vmem]),
        out_specs=vmem if ahead is None else [vmem, vmem],
        out_shape=out if ahead is None else [out, pltpu.VMEM((depth, width), bf16)],
        scratch_shapes=[pltpu.VMEM((depth, width), bf16), sems]
        + ([] if ahead is None else [sems]),
        compiler_params=params(24),
        cost_estimate=cost(2 * rows * depth * width, depth * width * 2),
        name="down",
    )(active, w_down, *([] if before is None else [before]))


BACK = ((2, 3), (0, 1))


def back_picks_kernel(layout, out):
    _, devices, _, rows = out.shape
    row = lax.broadcasted_iota(i32, (PAD, rows), 0)
    column = lax.broadcasted_iota(i32, (PAD, rows), 1)
    late = jnp.where(row < 8, row, jnp.where(row < LIVE_CAP, LIVE_CAP, row - (PAD - LIVE_CAP)))
    device = 0
    for core in (0, 1):
        for x in (2, 0):
            for masks in BACK:
                for mask in masks:
                    place = (x + core) * 4 + mask
                    base, count = layout[place], layout[devices + place]
                    for parity, rank in enumerate((row, late)):
                        mine = jnp.logical_and(column - rank == base, rank < count)
                        out[parity, device] = mine.astype(f32).astype(bf16)
                    device += 1


def back_picks(layout, rows):
    devices = layout.shape[0] // 2
    return pl.pallas_call(
        back_picks_kernel,
        in_specs=[pl.BlockSpec(memory_space=pltpu.SMEM)],
        out_specs=pl.BlockSpec(memory_space=pltpu.VMEM),
        out_shape=jax.ShapeDtypeStruct((2, devices, PAD, rows), bf16),
        compiler_params=params(16),
        name="back_picks",
    )(layout)


def down_unpack_kernel(picks_ref, a_ref, w_ref, before_ref, *refs):
    outs, wide = refs[:-1], refs[-1]
    rows = a_ref.shape[0]
    tiles, devices = wide.shape[:2]
    group = devices // len(outs)

    @pl.loop(0, tiles)
    def _(t):
        at = pl.ds(pl.multiple_of(t * DOWN_TILE, DOWN_TILE), DOWN_TILE)
        share = before_ref[:, at] + jnp.dot(a_ref[...], w_ref[:, at], preferred_element_type=f32)
        pick = picks_ref[lax.rem(t, 2)].reshape(devices * PAD, rows)
        back = jnp.dot(pick, share.astype(bf16), preferred_element_type=f32)
        wide[t] = back.reshape(devices, PAD, DOWN_TILE)

    per = tiles * LIVE_CAP
    for n, out in enumerate(outs):

        @pl.loop(0, group)
        def _(device):
            here = [wide[t, n * group + device] for t in range(tiles)]
            late = [here[t][8:] + here[t + 1][8:] for t in range(0, tiles, 2)]
            rows = pl.ds(pl.multiple_of(device * per, per), per)
            out[rows, :] = jnp.concatenate([h[:8] for h in here] + late, axis=0).astype(bf16)


def down_unpack(picks, active, weights, before):
    rows, depth = active.shape
    width = weights.shape[1]
    tiles, devices = width // DOWN_TILE, picks.shape[1]
    vmem = pl.BlockSpec(memory_space=pltpu.VMEM)
    out = jax.ShapeDtypeStruct((devices // 2 * tiles * LIVE_CAP, DOWN_TILE), bf16)
    return pl.pallas_call(
        down_unpack_kernel,
        in_specs=[vmem] * 4,
        out_specs=[vmem] * 2,
        out_shape=[out] * 2,
        scratch_shapes=[pltpu.VMEM((tiles, devices, PAD, DOWN_TILE), f32)],
        compiler_params=params(24),
        cost_estimate=cost(2 * rows * depth * width, rows * width * 4),
        name="down_unpack",
    )(picks, active, weights, before)


def finish_kernel(picks_ref, *refs):
    side = lax.axis_index("side")
    out_ref = refs[-1]
    sides = (len(refs) - 3) // 2
    mixed, squares, blocks = refs[:sides], refs[sides : sides + 2], refs[sides + 2 : -1]
    slots, width = out_ref.shape
    step = width // sides
    total = squares[0][...] + squares[1][...]
    root = lax.rsqrt(jnp.sum(total, axis=-1, keepdims=True) / width + epsilon)
    gain = root * root
    tiles = step // DOWN_TILE
    for shift in range(sides):
        base = (side ^ shift) * step
        block = blocks[shift][...]
        for t in range(tiles):
            back = jnp.dot(picks_ref[t], block, preferred_element_type=f32)[:slots]
            at = pl.multiple_of(base + t * DOWN_TILE, DOWN_TILE)
            here = mixed[shift][:, t * DOWN_TILE : (t + 1) * DOWN_TILE]
            out_ref[:, pl.ds(at, DOWN_TILE)] = (here + gain * back).astype(bf16)


def finish(picks, mixed, squares, blocks):
    vmem = pl.BlockSpec(memory_space=pltpu.VMEM)
    slots, width = mixed[0].shape[0], mixed[0].shape[1] * len(mixed)
    return pl.pallas_call(
        finish_kernel,
        in_specs=[vmem] * (2 * len(mixed) + 3),
        out_specs=vmem,
        out_shape=jax.ShapeDtypeStruct((slots, width), bf16),
        compiler_params=params(16),
        cost_estimate=cost(slots * width * 32, slots * width * 8),
        name="finish",
    )(picks, *mixed, *squares, *blocks)


def swap(x, axis, count, mask):
    return lax.ppermute(x, axis, [(j, j ^ mask) for j in range(count)])


def added(a, b):
    return (a.astype(f32) + b.astype(f32)).astype(bf16)


def tie(x, *others):
    return lax.optimization_barrier((x, *others))[0]


def squared_relu(*terms):
    lifted = sum(term.astype(f32) for term in terms)
    clipped = jnp.maximum(lifted, 0.0)
    return (clipped * clipped).astype(bf16)


def feed_forward(rows, layout, packed, other, w_up, w_down):
    half = w_up.shape[1] // 8
    across = lambda x: swap(x, "side", 4, 2)
    beside = lambda x: swap(x, "side", 4, 1)
    met_0 = beside(other[:rows])
    far = up(packed, w_up, rows, half, ((3, 1), (2, 0), (2, 1)))
    met_1 = beside(far[0])
    sum_0 = added(far[1], met_0)
    crossed_0 = across(sum_0)
    near = up(tie(packed, sum_0), w_up, rows, half, ((1, 0), (1, 1)))
    met_1, near = lax.optimization_barrier((met_1, near))
    sum_1 = added(far[2], met_1)
    crossed_1 = across(sum_1)
    near = beside(near)
    own, weights = up(tie(packed, sum_1), w_up, rows, half, ((0, 0), (0, 1)), w_down, ahead=3)
    active = [squared_relu(own[n], near[n], crossed) for n, crossed in enumerate((crossed_0, crossed_1))]
    active = jnp.concatenate(active, axis=1)
    over, following = across(active), beside(active)
    total = down(active, w_down, None, 0)
    picks = back_picks(tie(layout, total), rows)
    forward = beside(tie(over, picks))
    total = down(following, w_down, total, 1)
    total = down(over, w_down, total, 2)
    return down_unpack(picks, forward, weights, total)


ROW_STEPS = (112, 120, 128, 136, 144, 160, 192)


def line_shards(
    queries, new_kv, kv_pool, page_table, ctx_len, residual_in, norm_gain, w_up, w_down
):
    in_hbm = lambda x: pltpu.with_memory_space_constraint(x, pltpu.HBM)
    gain = norm_gain.reshape(-1, HEAD)
    inputs = queries, new_kv, kv_pool, page_table, ctx_len, residual_in, gain
    inputs, w_up, w_down = jax.tree.map(in_hbm, (inputs, w_up, w_down))
    (to_2, to_3), mixed_far, squares_far, copies = attend(inputs, 4, (2, 3), None)
    *copies, back_picks = copies
    met = swap(jnp.concatenate([to_2, to_3], axis=0), "side", 4, 2)
    (own, to_1), mixed_near, squares_near, _ = attend(inputs, 4, (0, 1), copies)
    first = jnp.concatenate([own, met[:TALL]], axis=0)
    second = swap(jnp.concatenate([to_1, met[TALL:]], axis=0), "side", 4, 1)
    gathered = []
    by_x = [swap(here, "shard", 4, 2) for here in (first, second)]
    by_core = [swap(here, "shard", 4, 1) for here in (first, second)]
    by_both = [swap(there, "shard", 4, 1) for there in by_x]
    gathered = [first, second, *by_core, *by_x, *by_both]
    packed, other, layout, step = pack_up(
        gathered, w_up, ROW_STEPS[-1], w_up.shape[1] // 8, 3, ROW_STEPS[:-1]
    )
    stay, leave = lax.switch(
        step[0],
        [functools.partial(feed_forward, rows) for rows in ROW_STEPS],
        layout, packed, other, w_up, w_down,
    )
    back = swap(leave, "shard", 4, 1)
    quarter = back.shape[0] // 4
    piece = quarter // 2
    cuts = [slice(at, at + quarter) for at in range(0, 4 * quarter, quarter)]
    sums = [added(stay[cut], back[cut]) for cut in cuts]
    far = added(sums[2], swap(sums[0], "shard", 4, 2))
    near = added(sums[3], swap(sums[1], "shard", 4, 2))
    home = near[:piece], near[piece:], far[:piece], far[piece:]
    blocks = [home[0]] + [swap(home[mask], "side", 4, mask) for mask in (1, 2, 3)]
    mixed = [*mixed_near, *mixed_far]
    return finish(back_picks, mixed, [squares_far, squares_near], blocks)


def attend_slots(queries, new_kv, pool_pages, page_rows, lengths):
    slot_count = queries.shape[0]
    positions = page_rows.shape[1] * pool_pages.shape[1]
    fetched = pool_pages[page_rows].reshape(slot_count, positions, 2, KV_HEADS, HEAD)
    fresh_kv = new_kv.reshape(slot_count, 2, KV_HEADS, HEAD)
    query_heads = queries.reshape(slot_count, KV_HEADS, GROUP, HEAD)
    score_scale = 1.0 / math.sqrt(HEAD)
    scores = (
        jnp.einsum("sgqd,slgd->sgql", query_heads, fetched[:, :, 0], preferred_element_type=f32)
        * score_scale
    )
    own_score = (
        jnp.einsum("sgqd,sgd->sgq", query_heads, fresh_kv[:, 0], preferred_element_type=f32)
        * score_scale
    )
    visible = (jnp.arange(positions, dtype=i32)[None, :] < lengths[:, None])[:, None, None, :]
    scores = jnp.where(visible, scores, -1e30)
    highest = jnp.maximum(jnp.max(scores, axis=-1), own_score)
    weights = jnp.where(visible, jnp.exp(scores - highest[..., None]), 0.0)
    own_weight = jnp.exp(own_score - highest)
    denominator = jnp.sum(weights, axis=-1) + own_weight
    probabilities = (weights / denominator[..., None]).astype(bf16)
    own_prob = (own_weight / denominator).astype(bf16).astype(f32)
    attended = jnp.einsum(
        "sgql,slgd->sgqd", probabilities, fetched[:, :, 1], preferred_element_type=f32
    )
    attended = attended + own_prob[..., None] * fresh_kv[:, 1].astype(f32)[:, :, None, :]
    return attended.reshape(slot_count, -1)


def any_shards(queries, new_kv, kv_pool, page_table, ctx_len, residual_in, norm_gain, w_up, w_down):
    attended = attend_slots(queries, new_kv, kv_pool, page_table, ctx_len)
    mixed_rows = residual_in.astype(f32) + attended
    mean_square = jnp.mean(mixed_rows * mixed_rows, axis=-1, keepdims=True)
    normed = (mixed_rows * lax.rsqrt(mean_square + epsilon) * norm_gain.astype(f32)).astype(bf16)
    live_mask = ctx_len > 0
    spread = lax.all_to_all(normed, "side", split_axis=1, concat_axis=0, tiled=True)
    up_partial = jnp.dot(
        lax.all_gather(spread, "shard", axis=0, tiled=True), w_up, preferred_element_type=f32
    )
    lifted = lax.psum(up_partial, "side")
    clipped = jnp.maximum(lifted, 0.0)
    active = (clipped * clipped).astype(bf16)
    down_share = lax.psum_scatter(
        jnp.dot(active, w_down, preferred_element_type=f32).astype(bf16),
        "shard",
        scatter_dimension=0,
        tiled=True,
    )
    returned = lax.all_to_all(down_share, "side", split_axis=0, concat_axis=1, tiled=True)
    returned = jnp.where(live_mask[:, None], returned.astype(f32), 0.0)
    return (mixed_rows + returned).astype(bf16)


def solution(mesh):
    rows = ("grp", "side", "shard")
    placed = (
        P(rows, None),
        P(rows, None),
        P(rows, None, None),
        P(rows, None),
        P(rows),
        P(rows, None),
        P(),
        P("side", "shard"),
        P("shard", "side"),
    )
    square = mesh.shape["side"] == 4 and mesh.shape["shard"] == 4
    return jax.shard_map(
        line_shards if square else any_shards,
        mesh=mesh,
        in_specs=placed,
        out_specs=P(rows, None),
        check_vma=False,
    )
```

profile of v0, /device:TPU:0, one launch (start us, length us, event | category | flops | bytes accessed | tf_op | source)
XLA Modules:
  0.0 91.5 jit_solution(12671654835640028773)
XLA Ops:
  0.0 5.6 %attend.2 = (bf16[24,1024]{1,0:T(8,128)(2,1)S(1)}, bf16[24,1024]{1,0:T(8,128)(2,1)S(1)}, f32[15,2048]{1,0:T(8,128)S(1)}, f32[15,2048]{1,0:T(8,128)S(1)}, f32[15,...) custom-call(s32[15]{0:T(128)} %refs_0_.1, ...), custom_call_target="tpu_custom_call" | custom-call | flops 31250000 | bytes 57344 | tf_op jit(solution)/shard_map/attend/pallas_call | solution.py:253
  5.6 4.1 %collective-permute-start.56 = (bf16[48,1024]{1,0:T(8,128)(2,1)S(1)}, bf16[48,1024]{1,0:T(8,128)(2,1)S(1)}, u32[]{:S(2)}, u32[]{:S(2)}) collective-permute-start(bf16[48,1024]{1,0:T(8,128)(2,1)S(1)} %pad_maximum_fusion.7), channel_id=1, source_target_pairs={{0,8},{4,12},{8,0},{12,4},{1,9},{5,13},{9,1},{13,5},{2,10},{6,14},... | collective-permute-start | bytes 294920 | tf_op jit(solution)/shard_map/ppermute | solution.py:609
  9.7 4.1 %attend.3 = (bf16[24,1024]{1,0:T(8,128)(2,1)S(1)}, bf16[24,1024]{1,0:T(8,128)(2,1)S(1)}, f32[15,2048]{1,0:T(8,128)S(1)}, f32[15,2048]{1,0:T(8,128)S(1)}, f32[15,128]{1,0:T(8,128)S(1)}) custom-call(bf16[15,8192]{1,0:T(8,128)(2,1)S(1)} %get-tuple-element.191.refs_0_, bf16[15,2048]{1,0:T(8,128)(2,1)S(1)} %get-tuple-element.192.refs_1_, ...), custom_call_target="tpu_custom_call" | custom-call | flops 31250000 | bytes 57344 | tf_op jit(solution)/shard_map/attend/pallas_call | solution.py:253
  13.8 0.8 collective-permute-done.56
  14.7 0.8 collective-permute-start.57
  15.5 1.6 %collective-permute-start.60 = (bf16[48,1024]{1,0:T(8,128)(2,1)S(1)}, bf16[48,1024]{1,0:T(8,128)(2,1)S(1)}, u32[]{:S(2)}, u32[]{:S(2)}) collective-permute-start(bf16[48,1024]{1,0:T(8,128)(2,1)S(1)} %pad_maximum_fusion.8.refs_0_), channel_id=1, source_target_pairs={{0,2},{1,3},{2,0},{3,1},{4,6},{5,7},{6,4},{7,5},{8,10},{9,11},{10,... | collective-permute-start | bytes 294920 | tf_op jit(solution)/shard_map/ppermute | solution.py:609
  17.0 2.3 %collective-permute-done.57.refs_1_ = bf16[48,1024]{1,0:T(8,128)(2,1)S(1)} collective-permute-done((bf16[48,1024]{1,0:T(8,128)(2,1)S(1)}, bf16[48,1024]{1,0:T(8,128)(2,1)S(1)}, u32[]{:S(2)}, u32[]{:S(2)}) %collective-permute-start.57) | collective-permute-done | bytes 98336 | tf_op jit(solution)/shard_map/ppermute | solution.py:609
  19.3 1.5 %collective-permute-start.61 = (bf16[48,1024]{1,0:T(8,128)(2,1)S(1)}, bf16[48,1024]{1,0:T(8,128)(2,1)S(1)}, u32[]{:S(2)}, u32[]{:S(2)}) collective-permute-start(bf16[48,1024]{1,0:T(8,128)(2,1)S(1)} %collective-permute-done.57.refs_1_), channel_id=1, source_target_pairs={{0,2},{1,3},{2,0},{3,1},{4,6},{5,7},{6,4},{7,5},{8,10},{9,11},{10,... | collective-permute-start | bytes 294920 | tf_op jit(solution)/shard_map/ppermute | solution.py:609
  20.8 0.5 collective-permute-start.59
  21.4 0.0 collective-permute-start.62
  21.4 2.6 %collective-permute-done.61.refs_5_ = bf16[48,1024]{1,0:T(8,128)(2,1)S(1)} collective-permute-done((bf16[48,1024]{1,0:T(8,128)(2,1)S(1)}, bf16[48,1024]{1,0:T(8,128)(2,1)S(1)}, u32[]{:S(2)}, u32[]{:S(2)}) %collective-permute-start.61) | collective-permute-done | bytes 98336 | tf_op jit(solution)/shard_map/ppermute | solution.py:609
  24.0 1.3 %collective-permute-done.63.refs_7_ = bf16[48,1024]{1,0:T(8,128)(2,1)S(1)} collective-permute-done((bf16[48,1024]{1,0:T(8,128)(2,1)S(1)}, bf16[48,1024]{1,0:T(8,128)(2,1)S(1)}, u32[]{:S(2)}, u32[]{:S(2)}) %collective-permute-start.63) | collective-permute-done | bytes 98336 | tf_op jit(solution)/shard_map/ppermute | solution.py:609
  25.3 2.6 %pack_up.1 = (bf16[192,2048]{1,0:T(8,128)(2,1)S(1)}, bf16[192,512]{1,0:T(8,128)(2,1)S(1)}, s32[32]{0:T(128)S(1)}, s32[1]{0:T(128)}) custom-call(bf16[48,1024]{1,0:T(8,128)(2,1)S(1)} %pad_maximum_fusion.8.refs_0_, bf16[48,1024]{1,0:T(8,128)(2,1)S(1)} %collective-permute-done.57.refs_1_, bf16[48,1024]{1,0:T(8,128)(2,1)S(1)} %collective-permute-done.58.refs_2_, ...), custom_call_target="tpu_custom_call" | custom-call | flops 6291456 | bytes 32768 | tf_op jit(solution)/shard_map/pack_up/pallas_call | solution.py:423
  28.6 44.1 %conditional.1 = ((bf16[384,512]{1,0:T(8,128)(2,1)S(1)}, bf16[384,512]{1,0:T(8,128)(2,1)S(1)})) conditional(s32[]{:T(128)} %bitcast.50, (bf16[192,2048]{1,0:T(8,128)(2,1)S(1)}, bf16[2048,4096]{1,0:T(8,128)(2,1)}, bf16[192,512]{1,0:T(8,128)(2,1)S(1)}, bf16[4096,2048]{1,0:T(8,128)(2,1)}, s32[32]{0:T(128)S(1)}) %tuple.61, ...), branch_computations={%region_0.0_spmd, %region_1.0_spmd, %region_2.0_spmd, %region_3.0_... | conditional | flops 72351744 | bytes 13820232 | solution.py:676
  28.8 0.9 collective-permute-start.17
  29.7 3.2 %up.27 = bf16[3,128,512]{2,1,0:T(8,128)(2,1)S(1)} custom-call(bf16[192,2048]{1,0:T(8,128)(2,1)S(1)} %get-tuple-element.107.x_ref, bf16[2048,4096]{1,0:T(8,128)(2,1)} %get-tuple-element.103.w_ref), custom_call_target="tpu_custom_call" | custom-call | flops 4194304 | bytes 98304 | tf_op jit(solution)/shard_map/cond/branch_2_fun/up/pallas_call | solution.py:330
  32.9 1.3 %collective-permute-start.16 = (bf16[128,512]{1,0:T(8,128)(2,1)S(1)}, bf16[128,512]{1,0:T(8,128)(2,1)S(1)}, u32[]{:S(2)}, u32[]{:S(2)}) collective-permute-start(bf16[128,512]{1,0:T(8,128)(2,1)S(1)} %slice_bitcast_fusion.7), channel_id=1, source_target_pairs={{0,4},{4,0},{8,12},{12,8},{1,5},{5,1},{9,13},{13,9},{2,6},{6,2},{1... | collective-permute-start | bytes 393224 | tf_op jit(solution)/shard_map/cond/branch_2_fun/ppermute | solution.py:609
  34.2 0.2 collective-permute-done.17
  34.4 2.5 %collective-permute-start.19 = (bf16[128,512]{1,0:T(8,128)(2,1)S(1)}, bf16[128,512]{1,0:T(8,128)(2,1)S(1)}, u32[]{:S(2)}, u32[]{:S(2)}) collective-permute-start(bf16[128,512]{1,0:T(8,128)(2,1)S(1)} %fusion.16), channel_id=1, source_target_pairs={{0,8},{4,12},{8,0},{12,4},{1,9},{5,13},{9,1},{13,5},{2,10},{6,14},... | collective-permute-start | bytes 393224 | tf_op jit(solution)/shard_map/cond/branch_2_fun/ppermute | solution.py:609
  37.0 2.6 %up.28 = bf16[2,128,512]{2,1,0:T(8,128)(2,1)S(1)} custom-call(bf16[192,2048]{1,0:T(8,128)(2,1)S(1)} %get-tuple-element.107.x_ref, bf16[2048,4096]{1,0:T(8,128)(2,1)} %get-tuple-element.103.w_ref), custom_call_target="tpu_custom_call" | custom-call | flops 4194304 | bytes 65536 | tf_op jit(solution)/shard_map/cond/branch_2_fun/up/pallas_call | solution.py:330
  39.6 1.5 %collective-permute-done.16 = bf16[128,512]{1,0:T(8,128)(2,1)S(1)} collective-permute-done((bf16[128,512]{1,0:T(8,128)(2,1)S(1)}, bf16[128,512]{1,0:T(8,128)(2,1)S(1)}, u32[]{:S(2)}, u32[]{:S(2)}) %collective-permute-start.16) | collective-permute-done | bytes 131104 | tf_op jit(solution)/shard_map/cond/branch_2_fun/ppermute | solution.py:609
  41.1 0.3 collective-permute-start.18
  41.4 1.5 %collective-permute-start.20 = (bf16[128,512]{1,0:T(8,128)(2,1)S(1)}, bf16[128,512]{1,0:T(8,128)(2,1)S(1)}, u32[]{:S(2)}, u32[]{:S(2)}) collective-permute-start(bf16[128,512]{1,0:T(8,128)(2,1)S(1)} %fusion.17), channel_id=1, source_target_pairs={{0,8},{4,12},{8,0},{12,4},{1,9},{5,13},{9,1},{13,5},{2,10},{6,14},... | collective-permute-start | bytes 393224 | tf_op jit(solution)/shard_map/cond/branch_2_fun/ppermute | solution.py:609
  42.9 3.6 %up.29 = (bf16[2,128,512]{2,1,0:T(8,128)(2,1)S(1)}, bf16[1024,2048]{1,0:T(8,128)(2,1)S(1)}) custom-call(bf16[192,2048]{1,0:T(8,128)(2,1)S(1)} %get-tuple-element.107.x_ref, bf16[2048,4096]{1,0:T(8,128)(2,1)} %get-tuple-element.103.w_ref, bf16[4096,2048]{1,0:T(8,128)(2,1)} %get-tuple-element.108.refs_0_.refs_1_), custom_call_target="tpu_custom_call" | custom-call | flops 4194304 | bytes 65536 | tf_op jit(solution)/shard_map/cond/branch_2_fun/up/pallas_call | solution.py:330
  46.5 2.6 %collective-permute-done.20 = bf16[128,512]{1,0:T(8,128)(2,1)S(1)} collective-permute-done((bf16[128,512]{1,0:T(8,128)(2,1)S(1)}, bf16[128,512]{1,0:T(8,128)(2,1)S(1)}, u32[]{:S(2)}, u32[]{:S(2)}) %collective-permute-start.20) | collective-permute-done | bytes 131104 | tf_op jit(solution)/shard_map/cond/branch_2_fun/ppermute | solution.py:609
  49.0 0.8 collective-permute-done.18
  49.9 0.1 fusion.23
  50.0 2.6 %collective-permute-start.21 = (bf16[128,1024]{1,0:T(8,128)(2,1)S(1)}, bf16[128,1024]{1,0:T(8,128)(2,1)S(1)}, u32[]{:S(2)}, u32[]{:S(2)}) collective-permute-start(bf16[128,1024]{1,0:T(8,128)(2,1)S(1)} %pad_maximum_fusion.2.refs_0_), channel_id=1, source_target_pairs={{0,8},{4,12},{8,0},{12,4},{1,9},{5,13},{9,1},{13,5},{2,10},{6,14},... | collective-permute-start | bytes 786440 | tf_op jit(solution)/shard_map/cond/branch_2_fun/ppermute | solution.py:609
  52.6 2.0 %collective-permute-start.23 = (bf16[128,1024]{1,0:T(8,128)(2,1)S(1)}, bf16[128,1024]{1,0:T(8,128)(2,1)S(1)}, u32[]{:S(2)}, u32[]{:S(2)}) collective-permute-start(bf16[128,1024]{1,0:T(8,128)(2,1)S(1)} %pad_maximum_fusion.2.refs_0_), channel_id=1, source_target_pairs={{0,4},{4,0},{8,12},{12,8},{1,5},{5,1},{9,13},{13,9},{2,6},{6,2},{1... | collective-permute-start | bytes 786440 | tf_op jit(solution)/shard_map/cond/branch_2_fun/ppermute | solution.py:609
  54.6 2.5 %down.27.refs_2_ = f32[128,2048]{1,0:T(8,128)S(1)} custom-call(bf16[128,1024]{1,0:T(8,128)(2,1)S(1)} %pad_maximum_fusion.2.refs_0_, bf16[4096,2048]{1,0:T(8,128)(2,1)} %get-tuple-element.108.refs_0_.refs_1_), custom_call_target="tpu_custom_call" | custom-call | flops 8388608 | bytes 65536 | tf_op jit(solution)/shard_map/cond/branch_2_fun/down/pallas_call | solution.py:483
  57.2 0.6 back_picks.9.picks_ref
  57.8 5.8 %collective-permute-done.21.refs_0_ = bf16[128,1024]{1,0:T(8,128)(2,1)S(1)} collective-permute-done((bf16[128,1024]{1,0:T(8,128)(2,1)S(1)}, bf16[128,1024]{1,0:T(8,128)(2,1)S(1)}, u32[]{:S(2)}, u32[]{:S(2)}) %collective-permute-start.21) | collective-permute-done | bytes 262176 | tf_op jit(solution)/shard_map/cond/branch_2_fun/ppermute | solution.py:609
  63.6 0.2 collective-permute-start.22
  63.8 2.6 %down.28.refs_2_ = f32[128,2048]{1,0:T(8,128)S(1)} custom-call(bf16[128,1024]{1,0:T(8,128)(2,1)S(1)} %collective-permute-done.23.refs_0_, bf16[4096,2048]{1,0:T(8,128)(2,1)} %get-tuple-element.108.refs_0_.refs_1_, f32[128,2048]{1,0:T(8,128)S(1)} %down.27.refs_2_), custom_call_target="tpu_custom_call" | custom-call | flops 8388608 | bytes 65536 | tf_op jit(solution)/shard_map/cond/branch_2_fun/down/pallas_call | solution.py:483
  66.3 2.6 %down.29.before_ref = f32[128,2048]{1,0:T(8,128)S(1)} custom-call(bf16[128,1024]{1,0:T(8,128)(2,1)S(1)} %collective-permute-done.21.refs_0_, bf16[4096,2048]{1,0:T(8,128)(2,1)} %get-tuple-element.108.refs_0_.refs_1_, f32[128,2048]{1,0:T(8,128)S(1)} %down.28.refs_2_), custom_call_target="tpu_custom_call" | custom-call | flops 8388608 | bytes 65536 | tf_op jit(solution)/shard_map/cond/branch_2_fun/down/pallas_call | solution.py:483
  68.9 1.3 %collective-permute-done.22.a_ref = bf16[128,1024]{1,0:T(8,128)(2,1)S(1)} collective-permute-done((bf16[128,1024]{1,0:T(8,128)(2,1)S(1)}, bf16[128,1024]{1,0:T(8,128)(2,1)S(1)}, u32[]{:S(2)}, u32[]{:S(2)}) %collective-permute-start.22) | collective-permute-done | bytes 262176 | tf_op jit(solution)/shard_map/cond/branch_2_fun/ppermute | solution.py:609
  70.2 2.2 %down_unpack.9 = (bf16[384,512]{1,0:T(8,128)(2,1)S(1)}, bf16[384,512]{1,0:T(8,128)(2,1)S(1)}) custom-call(bf16[2,16,16,128]{3,2,1,0:T(8,128)(2,1)S(1)} %back_picks.9.picks_ref, bf16[128,1024]{1,0:T(8,128)(2,1)S(1)} %collective-permute-done.22.a_ref, bf16[1024,2048]{1,0:T(8,128)(2,1)S(1)} %get-tuple-element.113.w_ref, f32[128,2048]{1,0:T(8,128)S(1)} %down.29.before_ref), custom_call_target="tpu_custom_call" | custom-call | flops 8388608 | bytes 16384 | tf_op jit(solution)/shard_map/cond/branch_2_fun/down_unpack/pallas_call | solution.py:561
  72.6 0.1 collective-permute-start.64
  72.7 1.7 %collective-permute-done.64 = bf16[384,512]{1,0:T(8,128)(2,1)S(1)} collective-permute-done((bf16[384,512]{1,0:T(8,128)(2,1)S(1)}, bf16[384,512]{1,0:T(8,128)(2,1)S(1)}, u32[]{:S(2)}, u32[]{:S(2)}) %collective-permute-start.64) | collective-permute-done | bytes 393248 | tf_op jit(solution)/shard_map/ppermute | solution.py:609
  74.5 1.5 %collective-permute-start.67 = (bf16[96,512]{1,0:T(8,128)(2,1)S(1)}, bf16[96,512]{1,0:T(8,128)(2,1)S(1)}, u32[]{:S(2)}, u32[]{:S(2)}) collective-permute-start(bf16[96,512]{1,0:T(8,128)(2,1)S(1)} %add_convert_fusion.1), channel_id=1, source_target_pairs={{0,2},{1,3},{2,0},{3,1},{4,6},{5,7},{6,4},{7,5},{8,10},{9,11},{10,... | collective-permute-start | bytes 294920 | tf_op jit(solution)/shard_map/ppermute | solution.py:609
  75.9 3.4 %collective-permute-done.67 = bf16[96,512]{1,0:T(8,128)(2,1)S(1)} collective-permute-done((bf16[96,512]{1,0:T(8,128)(2,1)S(1)}, bf16[96,512]{1,0:T(8,128)(2,1)S(1)}, u32[]{:S(2)}, u32[]{:S(2)}) %collective-permute-start.67) | collective-permute-done | bytes 98336 | tf_op jit(solution)/shard_map/ppermute | solution.py:609
  79.4 0.1 add_convert_fusion
  79.4 1.5 %collective-permute-start.65 = (bf16[96,512]{1,0:T(8,128)(2,1)S(1)}, bf16[96,512]{1,0:T(8,128)(2,1)S(1)}, u32[]{:S(2)}, u32[]{:S(2)}) collective-permute-start(bf16[96,512]{1,0:T(8,128)(2,1)S(1)} %get-tuple-element.229), channel_id=1, source_target_pairs={{0,2},{1,3},{2,0},{3,1},{4,6},{5,7},{6,4},{7,5},{8,10},{9,11},{10,... | collective-permute-start | bytes 294920 | tf_op jit(solution)/shard_map/ppermute | solution.py:609
  80.9 4.6 %collective-permute-start.69 = (bf16[48,512]{1,0:T(8,128)(2,1)S(1)}, bf16[48,512]{1,0:T(8,128)(2,1)S(1)}, u32[]{:S(2)}, u32[]{:S(2)}) collective-permute-start(bf16[48,512]{1,0:T(8,128)(2,1)S(1)} %get-tuple-element.230), channel_id=1, source_target_pairs={{0,12},{4,8},{8,4},{12,0},{1,13},{5,9},{9,5},{13,1},{2,14},{6,10},... | collective-permute-start | bytes 147464 | tf_op jit(solution)/shard_map/ppermute | solution.py:609
  85.6 0.7 collective-permute-start.66
  86.3 1.4 %collective-permute-done.69.refs_9_ = bf16[48,512]{1,0:T(8,128)(2,1)S(1)} collective-permute-done((bf16[48,512]{1,0:T(8,128)(2,1)S(1)}, bf16[48,512]{1,0:T(8,128)(2,1)S(1)}, u32[]{:S(2)}, u32[]{:S(2)}) %collective-permute-start.69) | collective-permute-done | bytes 49184 | tf_op jit(solution)/shard_map/ppermute | solution.py:609
  87.7 2.8 %collective-permute-done.68.refs_8_ = bf16[48,512]{1,0:T(8,128)(2,1)S(1)} collective-permute-done((bf16[48,512]{1,0:T(8,128)(2,1)S(1)}, bf16[48,512]{1,0:T(8,128)(2,1)S(1)}, u32[]{:S(2)}, u32[]{:S(2)}) %collective-permute-start.68) | collective-permute-done | bytes 49184 | tf_op jit(solution)/shard_map/ppermute | solution.py:609
  90.5 1.0 %finish.1 = bf16[15,8192]{1,0:T(8,128)(2,1)} custom-call(bf16[4,16,48]{2,1,0:T(8,128)(2,1)S(1)} %get-tuple-element.190.picks_ref, f32[15,2048]{1,0:T(8,128)S(1)} %get-tuple-element.198.refs_0_, f32[15,2048]{1,0:T(8,128)S(1)} %get-tuple-element.199.refs_1_, f32[15,2048]{1,0:T(8,128)S(1)} %get-tuple-element.200.refs_2_, ...), custom_call_target="tpu_custom_call" | custom-call | flops 61440 | bytes 15360 | tf_op jit(solution)/shard_map/finish/pallas_call | solution.py:597
  (24 shorter events, 0.2 us)
Async XLA Ops:
  5.6 9.0 %collective-permute-start.56 = (bf16[48,1024]{1,0:T(8,128)(2,1)S(1)}, bf16[48,1024]{1,0:T(8,128)(2,1)S(1)}, u32[]{:S(2)}, u32[]{:S(2)}) collective-permute-start(bf16[48,1024]{1,0:T(8,128)(2,1)S(1)} %pad_maximum_fusion.7), channel_id=1, source_target_pairs={{0,8},{4,12},{8,0},{12,4},{1,9},{5,13},{9,1},{13,5},{2,10},{6,14},... | collective-permute-start | bytes 294920 | tf_op jit(solution)/shard_map/ppermute | solution.py:609
  14.7 4.7 %collective-permute-start.57 = (bf16[48,1024]{1,0:T(8,128)(2,1)S(1)}, bf16[48,1024]{1,0:T(8,128)(2,1)S(1)}, u32[]{:S(2)}, u32[]{:S(2)}) collective-permute-start(bf16[48,1024]{1,0:T(8,128)(2,1)S(1)} %pad_maximum_fusion.9), channel_id=1, source_target_pairs={{0,4},{4,0},{8,12},{12,8},{1,5},{5,1},{9,13},{13,9},{2,6},{6,2},{1... | collective-permute-start | bytes 294920 | tf_op jit(solution)/shard_map/ppermute | solution.py:609
  15.5 5.9 %collective-permute-start.60 = (bf16[48,1024]{1,0:T(8,128)(2,1)S(1)}, bf16[48,1024]{1,0:T(8,128)(2,1)S(1)}, u32[]{:S(2)}, u32[]{:S(2)}) collective-permute-start(bf16[48,1024]{1,0:T(8,128)(2,1)S(1)} %pad_maximum_fusion.8.refs_0_), channel_id=1, source_target_pairs={{0,2},{1,3},{2,0},{3,1},{4,6},{5,7},{6,4},{7,5},{8,10},{9,11},{10,... | collective-permute-start | bytes 294920 | tf_op jit(solution)/shard_map/ppermute | solution.py:609
  19.3 4.6 %collective-permute-start.61 = (bf16[48,1024]{1,0:T(8,128)(2,1)S(1)}, bf16[48,1024]{1,0:T(8,128)(2,1)S(1)}, u32[]{:S(2)}, u32[]{:S(2)}) collective-permute-start(bf16[48,1024]{1,0:T(8,128)(2,1)S(1)} %collective-permute-done.57.refs_1_), channel_id=1, source_target_pairs={{0,2},{1,3},{2,0},{3,1},{4,6},{5,7},{6,4},{7,5},{8,10},{9,11},{10,... | collective-permute-start | bytes 294920 | tf_op jit(solution)/shard_map/ppermute | solution.py:609
  20.8 3.1 %collective-permute-start.58 = (bf16[48,1024]{1,0:T(8,128)(2,1)S(1)}, bf16[48,1024]{1,0:T(8,128)(2,1)S(1)}, u32[]{:S(2)}, u32[]{:S(2)}) collective-permute-start(bf16[48,1024]{1,0:T(8,128)(2,1)S(1)} %pad_maximum_fusion.8.refs_0_), channel_id=1, source_target_pairs={{0,1},{1,0},{2,3},{3,2},{4,5},{5,4},{6,7},{7,6},{8,9},{9,8},{10,11... | collective-permute-start | bytes 294920 | tf_op jit(solution)/shard_map/ppermute | solution.py:609
  20.8 3.1 %collective-permute-start.59 = (bf16[48,1024]{1,0:T(8,128)(2,1)S(1)}, bf16[48,1024]{1,0:T(8,128)(2,1)S(1)}, u32[]{:S(2)}, u32[]{:S(2)}) collective-permute-start(bf16[48,1024]{1,0:T(8,128)(2,1)S(1)} %collective-permute-done.57.refs_1_), channel_id=1, source_target_pairs={{0,1},{1,0},{2,3},{3,2},{4,5},{5,4},{6,7},{7,6},{8,9},{9,8},{10,11... | collective-permute-start | bytes 294920 | tf_op jit(solution)/shard_map/ppermute | solution.py:609
  21.4 2.6 %collective-permute-start.62 = (bf16[48,1024]{1,0:T(8,128)(2,1)S(1)}, bf16[48,1024]{1,0:T(8,128)(2,1)S(1)}, u32[]{:S(2)}, u32[]{:S(2)}) collective-permute-start(bf16[48,1024]{1,0:T(8,128)(2,1)S(1)} %collective-permute-done.60.refs_4_), channel_id=1, source_target_pairs={{0,1},{1,0},{2,3},{3,2},{4,5},{5,4},{6,7},{7,6},{8,9},{9,8},{10,11... | collective-permute-start | bytes 294920 | tf_op jit(solution)/shard_map/ppermute | solution.py:609
  24.0 1.3 %collective-permute-start.63 = (bf16[48,1024]{1,0:T(8,128)(2,1)S(1)}, bf16[48,1024]{1,0:T(8,128)(2,1)S(1)}, u32[]{:S(2)}, u32[]{:S(2)}) collective-permute-start(bf16[48,1024]{1,0:T(8,128)(2,1)S(1)} %collective-permute-done.61.refs_5_), channel_id=1, source_target_pairs={{0,1},{1,0},{2,3},{3,2},{4,5},{5,4},{6,7},{7,6},{8,9},{9,8},{10,11... | collective-permute-start | bytes 294920 | tf_op jit(solution)/shard_map/ppermute | solution.py:609
  28.8 5.6 %collective-permute-start.17 = (bf16[128,512]{1,0:T(8,128)(2,1)S(1)}, bf16[128,512]{1,0:T(8,128)(2,1)S(1)}, u32[]{:S(2)}, u32[]{:S(2)}) collective-permute-start(bf16[128,512]{1,0:T(8,128)(2,1)S(1)} %slice.157), channel_id=1, source_target_pairs={{0,4},{4,0},{8,12},{12,8},{1,5},{5,1},{9,13},{13,9},{2,6},{6,2},{1... | collective-permute-start | bytes 393224 | tf_op jit(solution)/shard_map/cond/branch_2_fun/ppermute | solution.py:609
  32.9 8.1 %collective-permute-start.16 = (bf16[128,512]{1,0:T(8,128)(2,1)S(1)}, bf16[128,512]{1,0:T(8,128)(2,1)S(1)}, u32[]{:S(2)}, u32[]{:S(2)}) collective-permute-start(bf16[128,512]{1,0:T(8,128)(2,1)S(1)} %slice_bitcast_fusion.7), channel_id=1, source_target_pairs={{0,4},{4,0},{8,12},{12,8},{1,5},{5,1},{9,13},{13,9},{2,6},{6,2},{1... | collective-permute-start | bytes 393224 | tf_op jit(solution)/shard_map/cond/branch_2_fun/ppermute | solution.py:609
  34.4 12.0 %collective-permute-start.19 = (bf16[128,512]{1,0:T(8,128)(2,1)S(1)}, bf16[128,512]{1,0:T(8,128)(2,1)S(1)}, u32[]{:S(2)}, u32[]{:S(2)}) collective-permute-start(bf16[128,512]{1,0:T(8,128)(2,1)S(1)} %fusion.16), channel_id=1, source_target_pairs={{0,8},{4,12},{8,0},{12,4},{1,9},{5,13},{9,1},{13,5},{2,10},{6,14},... | collective-permute-start | bytes 393224 | tf_op jit(solution)/shard_map/cond/branch_2_fun/ppermute | solution.py:609
  41.1 8.8 %collective-permute-start.18 = (bf16[2,128,512]{2,1,0:T(8,128)(2,1)S(1)}, bf16[2,128,512]{2,1,0:T(8,128)(2,1)S(1)}, u32[]{:S(2)}, u32[]{:S(2)}) collective-permute-start(bf16[2,128,512]{2,1,0:T(8,128)(2,1)S(1)} %up.28), channel_id=1, source_target_pairs={{0,4},{4,0},{8,12},{12,8},{1,5},{5,1},{9,13},{13,9},{2,6},{6,2},{1... | collective-permute-start | bytes 786440 | tf_op jit(solution)/shard_map/cond/branch_2_fun/ppermute | solution.py:609
  41.4 7.6 %collective-permute-start.20 = (bf16[128,512]{1,0:T(8,128)(2,1)S(1)}, bf16[128,512]{1,0:T(8,128)(2,1)S(1)}, u32[]{:S(2)}, u32[]{:S(2)}) collective-permute-start(bf16[128,512]{1,0:T(8,128)(2,1)S(1)} %fusion.17), channel_id=1, source_target_pairs={{0,8},{4,12},{8,0},{12,4},{1,9},{5,13},{9,1},{13,5},{2,10},{6,14},... | collective-permute-start | bytes 393224 | tf_op jit(solution)/shard_map/cond/branch_2_fun/ppermute | solution.py:609
  50.0 13.6 %collective-permute-start.21 = (bf16[128,1024]{1,0:T(8,128)(2,1)S(1)}, bf16[128,1024]{1,0:T(8,128)(2,1)S(1)}, u32[]{:S(2)}, u32[]{:S(2)}) collective-permute-start(bf16[128,1024]{1,0:T(8,128)(2,1)S(1)} %pad_maximum_fusion.2.refs_0_), channel_id=1, source_target_pairs={{0,8},{4,12},{8,0},{12,4},{1,9},{5,13},{9,1},{13,5},{2,10},{6,14},... | collective-permute-start | bytes 786440 | tf_op jit(solution)/shard_map/cond/branch_2_fun/ppermute | solution.py:609
  52.6 11.1 %collective-permute-start.23 = (bf16[128,1024]{1,0:T(8,128)(2,1)S(1)}, bf16[128,1024]{1,0:T(8,128)(2,1)S(1)}, u32[]{:S(2)}, u32[]{:S(2)}) collective-permute-start(bf16[128,1024]{1,0:T(8,128)(2,1)S(1)} %pad_maximum_fusion.2.refs_0_), channel_id=1, source_target_pairs={{0,4},{4,0},{8,12},{12,8},{1,5},{5,1},{9,13},{13,9},{2,6},{6,2},{1... | collective-permute-start | bytes 786440 | tf_op jit(solution)/shard_map/cond/branch_2_fun/ppermute | solution.py:609
  63.6 6.6 %collective-permute-start.22 = (bf16[128,1024]{1,0:T(8,128)(2,1)S(1)}, bf16[128,1024]{1,0:T(8,128)(2,1)S(1)}, u32[]{:S(2)}, u32[]{:S(2)}) collective-permute-start(bf16[128,1024]{1,0:T(8,128)(2,1)S(1)} %collective-permute-done.21.refs_0_), channel_id=1, source_target_pairs={{0,4},{4,0},{8,12},{12,8},{1,5},{5,1},{9,13},{13,9},{2,6},{6,2},{1... | collective-permute-start | bytes 786440 | tf_op jit(solution)/shard_map/cond/branch_2_fun/ppermute | solution.py:609
  72.6 1.8 %collective-permute-start.64 = (bf16[384,512]{1,0:T(8,128)(2,1)S(1)}, bf16[384,512]{1,0:T(8,128)(2,1)S(1)}, u32[]{:S(2)}, u32[]{:S(2)}) collective-permute-start(bf16[384,512]{1,0:T(8,128)(2,1)S(1)} %get-tuple-element.213), channel_id=1, source_target_pairs={{0,1},{1,0},{2,3},{3,2},{4,5},{5,4},{6,7},{7,6},{8,9},{9,8},{10,11... | collective-permute-start | bytes 1179656 | tf_op jit(solution)/shard_map/ppermute | solution.py:609
  74.5 4.9 %collective-permute-start.67 = (bf16[96,512]{1,0:T(8,128)(2,1)S(1)}, bf16[96,512]{1,0:T(8,128)(2,1)S(1)}, u32[]{:S(2)}, u32[]{:S(2)}) collective-permute-start(bf16[96,512]{1,0:T(8,128)(2,1)S(1)} %add_convert_fusion.1), channel_id=1, source_target_pairs={{0,2},{1,3},{2,0},{3,1},{4,6},{5,7},{6,4},{7,5},{8,10},{9,11},{10,... | collective-permute-start | bytes 294920 | tf_op jit(solution)/shard_map/ppermute | solution.py:609
  79.4 6.1 %collective-permute-start.65 = (bf16[96,512]{1,0:T(8,128)(2,1)S(1)}, bf16[96,512]{1,0:T(8,128)(2,1)S(1)}, u32[]{:S(2)}, u32[]{:S(2)}) collective-permute-start(bf16[96,512]{1,0:T(8,128)(2,1)S(1)} %get-tuple-element.229), channel_id=1, source_target_pairs={{0,2},{1,3},{2,0},{3,1},{4,6},{5,7},{6,4},{7,5},{8,10},{9,11},{10,... | collective-permute-start | bytes 294920 | tf_op jit(solution)/shard_map/ppermute | solution.py:609
  80.9 6.8 %collective-permute-start.69 = (bf16[48,512]{1,0:T(8,128)(2,1)S(1)}, bf16[48,512]{1,0:T(8,128)(2,1)S(1)}, u32[]{:S(2)}, u32[]{:S(2)}) collective-permute-start(bf16[48,512]{1,0:T(8,128)(2,1)S(1)} %get-tuple-element.230), channel_id=1, source_target_pairs={{0,12},{4,8},{8,4},{12,0},{1,13},{5,9},{9,5},{13,1},{2,14},{6,10},... | collective-permute-start | bytes 147464 | tf_op jit(solution)/shard_map/ppermute | solution.py:609
  85.5 5.0 %collective-permute-start.68 = (bf16[48,512]{1,0:T(8,128)(2,1)S(1)}, bf16[48,512]{1,0:T(8,128)(2,1)S(1)}, u32[]{:S(2)}, u32[]{:S(2)}) collective-permute-start(bf16[48,512]{1,0:T(8,128)(2,1)S(1)} %get-tuple-element.231), channel_id=1, source_target_pairs={{0,8},{4,12},{8,0},{12,4},{1,9},{5,13},{9,1},{13,5},{2,10},{6,14},... | collective-permute-start | bytes 147464 | tf_op jit(solution)/shard_map/ppermute | solution.py:609
  85.6 4.9 %collective-permute-start.66 = (bf16[48,512]{1,0:T(8,128)(2,1)S(1)}, bf16[48,512]{1,0:T(8,128)(2,1)S(1)}, u32[]{:S(2)}, u32[]{:S(2)}) collective-permute-start(bf16[48,512]{1,0:T(8,128)(2,1)S(1)} %get-tuple-element.232), channel_id=1, source_target_pairs={{0,4},{4,0},{8,12},{12,8},{1,5},{5,1},{9,13},{13,9},{2,6},{6,2},{1... | collective-permute-start | bytes 147464 | tf_op jit(solution)/shard_map/ppermute | solution.py:609
where the time goes:
time: 92.7 us; the launch traced here: 91.5 us
  Pallas kernels  33.1 us (36%)
  waiting for transfers between devices  28.6 us (31%)
  starting transfers between devices  28.1 us (30%)
    ppermute x22, waiting for transfers between devices, swap(): return lax.ppermute(x, axis, [(j, j ^ mask) for j in range(count)])  28.6 us
    ppermute x22, starting transfers between devices, swap(): return lax.ppermute(x, axis, [(j, j ^ mask) for j in range(count)])  28.1 us
    pallas_call x2, Pallas kernels, attend(): pl.pallas_call(functools.partial(attend_kernel, masks=masks, sides=sides,...  9.63 us
    pallas_call x3, Pallas kernels, up(): pl.pallas_call(functools.partial(up_kernel, masks=masks, ahead=ahead), in...  9.39 us
    pallas_call x3, Pallas kernels, down(): pl.pallas_call(functools.partial(down_kernel, first=before is None, mask=...  7.67 us
    pallas_call x1, Pallas kernels, pack_up(): pl.pallas_call(functools.partial(pack_up_kernel, mask=mask, limits=limits...  2.65 us
    pallas_call x1, Pallas kernels, down_unpack(): pl.pallas_call(down_unpack_kernel, in_specs=[vmem] * 4, out_specs=[vmem]...  2.24 us
  transfers between devices with their start and end apart: 22, of which 14 were waited for; matrix products, arithmetic and copies ran while one was open for 0% of the time, Pallas kernels for 24%

commit v1 on v0

--- a/solution.py
+++ b/solution.py
@@ -101,12 +101,20 @@
     else:
         q_ref, new_ref, res_ref, gain_ref, bias_ref, picks_ref, empty_ref = take(7)
     pool_source = refs.pop(0)
+    w_ref = None if first else refs.pop(0)
     sends, mixed_refs = take(len(masks)), take(len(masks))
     square_ref = refs.pop(0)
+    weights_ref = None if first else refs.pop(0)
     if first:
         q_ref, new_ref, res_ref, gain_ref, bias_ref, picks_ref, empty_ref, back_ref = take(8)
         gain_copy, sems = take(2)
-    pool_ref, pool_sems = refs
+    pool_ref, pool_sems = take(2)
+    fetched = []
+    if not first:
+        rows, across = weights_ref.shape
+        column = pl.multiple_of((side ^ FIRST_BLOCK) * 2 * across, across)
+        for t in range(across // UP_TILE):
+            fetched.append(tile_copy(w_ref, 0, rows, column, weights_ref, refs[0], t, UP_TILE))
     slots, step = mixed_refs[0].shape
     pages, page, width = pool_source.shape
     columns = width // 2 // sides
@@ -155,6 +163,8 @@
     for copy in brought[0]:
         copy.wait()
     values_to_come = brought[1]
+    for copy in fetched:
+        copy.start()
 
     squares = jnp.zeros((slots, HEAD), f32)
     bias = bias_ref[...][None]
@@ -214,9 +224,14 @@
                 rows = jnp.where(empty_ref[...] > 0, EMPTY, rows)
             sends[job[0]][:, to] = rows.astype(bf16)
     square_ref[...] = squares
-
-
-def attend(inputs, sides, masks, before):
+    for copy in fetched:
+        copy.wait()
+
+
+FIRST_BLOCK = 3
+
+
+def attend(inputs, sides, masks, before, w_up):
     queries, new_kv, kv_pool, page_table, ctx_len, residual_in, norm_gain = inputs
     slots, columns = queries.shape
     pages, page, _ = kv_pool.shape
@@ -243,13 +258,17 @@
         ]
         scratch = [pltpu.VMEM(norm_gain.shape, bf16), pltpu.SemaphoreType.DMA((4,))]
     else:
-        operands = [*before, kv_pool]
-        in_specs = [vmem] * len(before) + [anywhere]
+        operands = [*before, kv_pool, w_up]
+        in_specs = [vmem] * len(before) + [anywhere] * 2
+        half = w_up.shape[1] // 8
+        out_shape.append(pltpu.VMEM((w_up.shape[0], half), bf16))
         scratch = []
     scratch += [
         pltpu.VMEM((pages, page, kv_pool.shape[2] // sides * 2), bf16),
         pltpu.SemaphoreType.DMA((2, POOL_CUTS)),
     ]
+    if not first:
+        scratch.append(pltpu.SemaphoreType.DMA((half // UP_TILE,)))
     outs = pl.pallas_call(
         functools.partial(attend_kernel, masks=masks, sides=sides, first=first),
         in_specs=in_specs,
@@ -370,17 +389,9 @@
     step_ref[0] = step
 
 
-def pack_up_kernel(*refs, mask, limits):
-    gathered, refs = refs[:-7], refs[-7:]
-    w_ref, packed_ref, out_ref, layout, step_ref, buffer, sems = refs
+def pack_up_kernel(*refs, limits):
+    gathered, (w_ref, packed_ref, out_ref, layout, step_ref) = refs[:-5], refs[-5:]
     width = out_ref.shape[1]
-
-    def copy_of(t):
-        column = pl.multiple_of((lax.axis_index("side") ^ mask) * 2 * width, width)
-        return tile_copy(w_ref, 0, buffer.shape[0], column, buffer, sems, t, UP_TILE)
-
-    for t in range(width // UP_TILE):
-        copy_of(t).start()
     find_layout(gathered, layout, step_ref, limits)
     rows, depth = packed_ref.shape
     per = gathered[0].shape[0]
@@ -409,20 +420,19 @@
 
     @pl.loop(0, width // UP_TILE)
     def _(t):
-        copy_of(t).wait()
         at = pl.ds(pl.multiple_of(t * UP_TILE, UP_TILE), UP_TILE)
         out_ref[:, at] = jnp.dot(
-            packed_ref[...], buffer[:, at], preferred_element_type=f32
+            packed_ref[...], w_ref[:, at], preferred_element_type=f32
         ).astype(bf16)
 
 
-def pack_up(gathered, w_up, rows, width, mask, limits):
-    depth = w_up.shape[0]
+def pack_up(gathered, weights, rows, limits):
+    depth, width = weights.shape
     devices = len(gathered) * gathered[0].shape[0] // TALL
     vmem, smem = pl.BlockSpec(memory_space=pltpu.VMEM), pl.BlockSpec(memory_space=pltpu.SMEM)
     return pl.pallas_call(
-        functools.partial(pack_up_kernel, mask=mask, limits=limits),
-        in_specs=[vmem] * len(gathered) + [pl.BlockSpec(memory_space=pl.ANY)],
+        functools.partial(pack_up_kernel, limits=limits),
+        in_specs=[vmem] * (len(gathered) + 1),
         out_specs=[vmem, vmem, smem, smem],
         out_shape=[
             jax.ShapeDtypeStruct((rows, depth), bf16),
@@ -430,14 +440,10 @@
             jax.ShapeDtypeStruct((2 * devices,), i32),
             jax.ShapeDtypeStruct((1,), i32),
         ],
-        scratch_shapes=[
-            pltpu.VMEM((depth, width), bf16),
-            pltpu.SemaphoreType.DMA((width // UP_TILE,)),
-        ],
         compiler_params=params(24),
         cost_estimate=cost(2 * rows * depth * width, depth * width * 2),
         name="pack_up",
-    )(*gathered, w_up)
+    )(*gathered, weights)
 
 
 def down_kernel(*refs, first, mask, ahead):
@@ -659,10 +665,10 @@
     gain = norm_gain.reshape(-1, HEAD)
     inputs = queries, new_kv, kv_pool, page_table, ctx_len, residual_in, gain
     inputs, w_up, w_down = jax.tree.map(in_hbm, (inputs, w_up, w_down))
-    (to_2, to_3), mixed_far, squares_far, copies = attend(inputs, 4, (2, 3), None)
+    (to_2, to_3), mixed_far, squares_far, copies = attend(inputs, 4, (2, 3), None, w_up)
     *copies, back_picks = copies
     met = swap(jnp.concatenate([to_2, to_3], axis=0), "side", 4, 2)
-    (own, to_1), mixed_near, squares_near, _ = attend(inputs, 4, (0, 1), copies)
+    (own, to_1), mixed_near, squares_near, (weights,) = attend(inputs, 4, (0, 1), copies, w_up)
     first = jnp.concatenate([own, met[:TALL]], axis=0)
     second = swap(jnp.concatenate([to_1, met[TALL:]], axis=0), "side", 4, 1)
     gathered = []
@@ -671,7 +677,7 @@
     by_both = [swap(there, "shard", 4, 1) for there in by_x]
     gathered = [first, second, *by_core, *by_x, *by_both]
     packed, other, layout, step = pack_up(
-        gathered, w_up, ROW_STEPS[-1], w_up.shape[1] // 8, 3, ROW_STEPS[:-1]
+        gathered, weights, ROW_STEPS[-1], ROW_STEPS[:-1]
     )
     stay, leave = lax.switch(
         step[0],

time: 92.7 us -> 91.9 us (level)
  the two profiles are of different devices: /device:TPU:0 before, /device:TPU:4 now
where the time goes in v1:
time: 91.9 us; the launch traced here: 90.1 us
  Pallas kernels  33.2 us (36%)
  waiting for transfers between devices  28.4 us (31%)
  starting transfers between devices  26.8 us (29%)
    ppermute x22, waiting for transfers between devices, swap(): return lax.ppermute(x, axis, [(j, j ^ mask) for j in range(count)])  28.4 us
    ppermute x22, starting transfers between devices, swap(): return lax.ppermute(x, axis, [(j, j ^ mask) for j in range(count)])  26.8 us
    pallas_call x2, Pallas kernels, attend(): pl.pallas_call(functools.partial(attend_kernel, masks=masks, sides=sides,...  9.65 us
    pallas_call x3, Pallas kernels, up(): pl.pallas_call(functools.partial(up_kernel, masks=masks, ahead=ahead), in...  9.39 us
    pallas_call x3, Pallas kernels, down(): pl.pallas_call(functools.partial(down_kernel, first=before is None, mask=...  7.67 us
    pallas_call x1, Pallas kernels, pack_up(): pl.pallas_call(functools.partial(pack_up_kernel, limits=limits), in_specs...  2.71 us
    pallas_call x1, Pallas kernels, down_unpack(): pl.pallas_call(down_unpack_kernel, in_specs=[vmem] * 4, out_specs=[vmem]...  2.24 us
  transfers between devices with their start and end apart: 22, of which 14 were waited for; matrix products, arithmetic and copies ran while one was open for 0% of the time, Pallas kernels for 24%

profile of v1, /device:TPU:4, one launch (start us, length us, event | category | flops | bytes accessed | tf_op | source)
XLA Modules:
  0.0 90.1 jit_solution(7026941798609885264)
XLA Ops:
  0.0 5.6 %attend.2 = (bf16[24,1024]{1,0:T(8,128)(2,1)S(1)}, bf16[24,1024]{1,0:T(8,128)(2,1)S(1)}, f32[15,2048]{1,0:T(8,128)S(1)}, f32[15,2048]{1,0:T(8,128)S(1)}, f32[15,...) custom-call(s32[15]{0:T(128)} %refs_0_.1, ...), custom_call_target="tpu_custom_call" | custom-call | flops 31250000 | bytes 57344 | tf_op jit(solution)/shard_map/attend/pallas_call | solution.py:272
  5.6 2.7 %collective-permute-start.56 = (bf16[48,1024]{1,0:T(8,128)(2,1)S(1)}, bf16[48,1024]{1,0:T(8,128)(2,1)S(1)}, u32[]{:S(2)}, u32[]{:S(2)}) collective-permute-start(bf16[48,1024]{1,0:T(8,128)(2,1)S(1)} %pad_maximum_fusion.7), channel_id=1, source_target_pairs={{0,8},{4,12},{8,0},{12,4},{1,9},{5,13},{9,1},{13,5},{2,10},{6,14},... | collective-permute-start | bytes 294920 | tf_op jit(solution)/shard_map/ppermute | solution.py:615
  8.3 4.1 %attend.3 = (bf16[24,1024]{1,0:T(8,128)(2,1)S(1)}, bf16[24,1024]{1,0:T(8,128)(2,1)S(1)}, f32[15,2048]{1,0:T(8,128)S(1)}, f32[15,2048]{1,0:T(8,128)S(1)}, f32[15,...) custom-call(bf16[15,8192]{1,0:T(8,128)(2,1)S(1)} %get-tuple-element.192.refs_0_, ...), custom_call_target="tpu_custom_call" | custom-call | flops 31250000 | bytes 57344 | tf_op jit(solution)/shard_map/attend/pallas_call | solution.py:272
  12.4 0.8 collective-permute-done.56
  13.2 0.8 collective-permute-start.57
  14.0 1.6 %collective-permute-start.60 = (bf16[48,1024]{1,0:T(8,128)(2,1)S(1)}, bf16[48,1024]{1,0:T(8,128)(2,1)S(1)}, u32[]{:S(2)}, u32[]{:S(2)}) collective-permute-start(bf16[48,1024]{1,0:T(8,128)(2,1)S(1)} %pad_maximum_fusion.8.refs_0_), channel_id=1, source_target_pairs={{0,2},{1,3},{2,0},{3,1},{4,6},{5,7},{6,4},{7,5},{8,10},{9,11},{10,... | collective-permute-start | bytes 294920 | tf_op jit(solution)/shard_map/ppermute | solution.py:615
  15.6 2.3 %collective-permute-done.57.refs_1_ = bf16[48,1024]{1,0:T(8,128)(2,1)S(1)} collective-permute-done((bf16[48,1024]{1,0:T(8,128)(2,1)S(1)}, bf16[48,1024]{1,0:T(8,128)(2,1)S(1)}, u32[]{:S(2)}, u32[]{:S(2)}) %collective-permute-start.57) | collective-permute-done | bytes 98336 | tf_op jit(solution)/shard_map/ppermute | solution.py:615
  17.9 1.5 %collective-permute-start.61 = (bf16[48,1024]{1,0:T(8,128)(2,1)S(1)}, bf16[48,1024]{1,0:T(8,128)(2,1)S(1)}, u32[]{:S(2)}, u32[]{:S(2)}) collective-permute-start(bf16[48,1024]{1,0:T(8,128)(2,1)S(1)} %collective-permute-done.57.refs_1_), channel_id=1, source_target_pairs={{0,2},{1,3},{2,0},{3,1},{4,6},{5,7},{6,4},{7,5},{8,10},{9,11},{10,... | collective-permute-start | bytes 294920 | tf_op jit(solution)/shard_map/ppermute | solution.py:615
  19.4 0.5 collective-permute-start.59
  19.9 0.0 collective-permute-start.62
  19.9 2.6 %collective-permute-done.61.refs_5_ = bf16[48,1024]{1,0:T(8,128)(2,1)S(1)} collective-permute-done((bf16[48,1024]{1,0:T(8,128)(2,1)S(1)}, bf16[48,1024]{1,0:T(8,128)(2,1)S(1)}, u32[]{:S(2)}, u32[]{:S(2)}) %collective-permute-start.61) | collective-permute-done | bytes 98336 | tf_op jit(solution)/shard_map/ppermute | solution.py:615
  22.5 1.3 %collective-permute-done.63.refs_7_ = bf16[48,1024]{1,0:T(8,128)(2,1)S(1)} collective-permute-done((bf16[48,1024]{1,0:T(8,128)(2,1)S(1)}, bf16[48,1024]{1,0:T(8,128)(2,1)S(1)}, u32[]{:S(2)}, u32[]{:S(2)}) %collective-permute-start.63) | collective-permute-done | bytes 98336 | tf_op jit(solution)/shard_map/ppermute | solution.py:615
  23.8 2.7 %pack_up.1 = (bf16[192,2048]{1,0:T(8,128)(2,1)S(1)}, bf16[192,512]{1,0:T(8,128)(2,1)S(1)}, s32[32]{0:T(128)S(1)}, s32[1]{0:T(128)}) custom-call(bf16[48,1024]{1,0:T(8,128)(2,1)S(1)} %pad_maximum_fusion.8.refs_0_, bf16[48,1024]{1,0:T(8,128)(2,1)S(1)} %collective-permute-done.57.refs_1_, bf16[48,1024]{1,0:T(8,128)(2,1)S(1)} %collective-permute-done.58.refs_2_, ...), custom_call_target="tpu_custom_call" | custom-call | flops 6291456 | bytes 32768 | tf_op jit(solution)/shard_map/pack_up/pallas_call | solution.py:433
  27.2 44.0 %conditional.1 = ((bf16[384,512]{1,0:T(8,128)(2,1)S(1)}, bf16[384,512]{1,0:T(8,128)(2,1)S(1)})) conditional(s32[]{:T(128)} %bitcast.50, (bf16[192,2048]{1,0:T(8,128)(2,1)S(1)}, bf16[2048,4096]{1,0:T(8,128)(2,1)}, bf16[192,512]{1,0:T(8,128)(2,1)S(1)}, bf16[4096,2048]{1,0:T(8,128)(2,1)}, s32[32]{0:T(128)S(1)}) %tuple.61, ...), branch_computations={%region_0.0_spmd, %region_1.0_spmd, %region_2.0_spmd, %region_3.0_... | conditional | flops 72351744 | bytes 13820232 | solution.py:682
  27.4 0.9 collective-permute-start.17
  28.3 3.2 %up.27 = bf16[3,128,512]{2,1,0:T(8,128)(2,1)S(1)} custom-call(bf16[192,2048]{1,0:T(8,128)(2,1)S(1)} %get-tuple-element.107.x_ref, bf16[2048,4096]{1,0:T(8,128)(2,1)} %get-tuple-element.103.w_ref), custom_call_target="tpu_custom_call" | custom-call | flops 4194304 | bytes 98304 | tf_op jit(solution)/shard_map/cond/branch_2_fun/up/pallas_call | solution.py:349
  31.6 1.3 %collective-permute-start.16 = (bf16[128,512]{1,0:T(8,128)(2,1)S(1)}, bf16[128,512]{1,0:T(8,128)(2,1)S(1)}, u32[]{:S(2)}, u32[]{:S(2)}) collective-permute-start(bf16[128,512]{1,0:T(8,128)(2,1)S(1)} %slice_bitcast_fusion.7), channel_id=1, source_target_pairs={{0,4},{4,0},{8,12},{12,8},{1,5},{5,1},{9,13},{13,9},{2,6},{6,2},{1... | collective-permute-start | bytes 393224 | tf_op jit(solution)/shard_map/cond/branch_2_fun/ppermute | solution.py:615
  32.9 0.2 collective-permute-done.17
  33.1 2.5 %collective-permute-start.19 = (bf16[128,512]{1,0:T(8,128)(2,1)S(1)}, bf16[128,512]{1,0:T(8,128)(2,1)S(1)}, u32[]{:S(2)}, u32[]{:S(2)}) collective-permute-start(bf16[128,512]{1,0:T(8,128)(2,1)S(1)} %fusion.16), channel_id=1, source_target_pairs={{0,8},{4,12},{8,0},{12,4},{1,9},{5,13},{9,1},{13,5},{2,10},{6,14},... | collective-permute-start | bytes 393224 | tf_op jit(solution)/shard_map/cond/branch_2_fun/ppermute | solution.py:615
  35.6 2.6 %up.28 = bf16[2,128,512]{2,1,0:T(8,128)(2,1)S(1)} custom-call(bf16[192,2048]{1,0:T(8,128)(2,1)S(1)} %get-tuple-element.107.x_ref, bf16[2048,4096]{1,0:T(8,128)(2,1)} %get-tuple-element.103.w_ref), custom_call_target="tpu_custom_call" | custom-call | flops 4194304 | bytes 65536 | tf_op jit(solution)/shard_map/cond/branch_2_fun/up/pallas_call | solution.py:349
  38.2 1.5 %collective-permute-done.16 = bf16[128,512]{1,0:T(8,128)(2,1)S(1)} collective-permute-done((bf16[128,512]{1,0:T(8,128)(2,1)S(1)}, bf16[128,512]{1,0:T(8,128)(2,1)S(1)}, u32[]{:S(2)}, u32[]{:S(2)}) %collective-permute-start.16) | collective-permute-done | bytes 131104 | tf_op jit(solution)/shard_map/cond/branch_2_fun/ppermute | solution.py:615
  39.7 0.3 collective-permute-start.18
  40.0 1.5 %collective-permute-start.20 = (bf16[128,512]{1,0:T(8,128)(2,1)S(1)}, bf16[128,512]{1,0:T(8,128)(2,1)S(1)}, u32[]{:S(2)}, u32[]{:S(2)}) collective-permute-start(bf16[128,512]{1,0:T(8,128)(2,1)S(1)} %fusion.17), channel_id=1, source_target_pairs={{0,8},{4,12},{8,0},{12,4},{1,9},{5,13},{9,1},{13,5},{2,10},{6,14},... | collective-permute-start | bytes 393224 | tf_op jit(solution)/shard_map/cond/branch_2_fun/ppermute | solution.py:615
  41.5 3.6 %up.29 = (bf16[2,128,512]{2,1,0:T(8,128)(2,1)S(1)}, bf16[1024,2048]{1,0:T(8,128)(2,1)S(1)}) custom-call(bf16[192,2048]{1,0:T(8,128)(2,1)S(1)} %get-tuple-element.107.x_ref, bf16[2048,4096]{1,0:T(8,128)(2,1)} %get-tuple-element.103.w_ref, bf16[4096,2048]{1,0:T(8,128)(2,1)} %get-tuple-element.108.refs_0_.refs_1_), custom_call_target="tpu_custom_call" | custom-call | flops 4194304 | bytes 65536 | tf_op jit(solution)/shard_map/cond/branch_2_fun/up/pallas_call | solution.py:349
  45.1 2.6 %collective-permute-done.20 = bf16[128,512]{1,0:T(8,128)(2,1)S(1)} collective-permute-done((bf16[128,512]{1,0:T(8,128)(2,1)S(1)}, bf16[128,512]{1,0:T(8,128)(2,1)S(1)}, u32[]{:S(2)}, u32[]{:S(2)}) %collective-permute-start.20) | collective-permute-done | bytes 131104 | tf_op jit(solution)/shard_map/cond/branch_2_fun/ppermute | solution.py:615
  47.7 0.8 collective-permute-done.18
  48.5 0.1 fusion.23
  48.6 2.6 %collective-permute-start.21 = (bf16[128,1024]{1,0:T(8,128)(2,1)S(1)}, bf16[128,1024]{1,0:T(8,128)(2,1)S(1)}, u32[]{:S(2)}, u32[]{:S(2)}) collective-permute-start(bf16[128,1024]{1,0:T(8,128)(2,1)S(1)} %pad_maximum_fusion.2.refs_0_), channel_id=1, source_target_pairs={{0,8},{4,12},{8,0},{12,4},{1,9},{5,13},{9,1},{13,5},{2,10},{6,14},... | collective-permute-start | bytes 786440 | tf_op jit(solution)/shard_map/cond/branch_2_fun/ppermute | solution.py:615
  51.3 1.9 %collective-permute-start.23 = (bf16[128,1024]{1,0:T(8,128)(2,1)S(1)}, bf16[128,1024]{1,0:T(8,128)(2,1)S(1)}, u32[]{:S(2)}, u32[]{:S(2)}) collective-permute-start(bf16[128,1024]{1,0:T(8,128)(2,1)S(1)} %pad_maximum_fusion.2.refs_0_), channel_id=1, source_target_pairs={{0,4},{4,0},{8,12},{12,8},{1,5},{5,1},{9,13},{13,9},{2,6},{6,2},{1... | collective-permute-start | bytes 786440 | tf_op jit(solution)/shard_map/cond/branch_2_fun/ppermute | solution.py:615
  53.2 2.6 %down.27.refs_2_ = f32[128,2048]{1,0:T(8,128)S(1)} custom-call(bf16[128,1024]{1,0:T(8,128)(2,1)S(1)} %pad_maximum_fusion.2.refs_0_, bf16[4096,2048]{1,0:T(8,128)(2,1)} %get-tuple-element.108.refs_0_.refs_1_), custom_call_target="tpu_custom_call" | custom-call | flops 8388608 | bytes 65536 | tf_op jit(solution)/shard_map/cond/branch_2_fun/down/pallas_call | solution.py:489
  55.8 0.6 back_picks.9.picks_ref
  56.4 5.8 %collective-permute-done.21.refs_0_ = bf16[128,1024]{1,0:T(8,128)(2,1)S(1)} collective-permute-done((bf16[128,1024]{1,0:T(8,128)(2,1)S(1)}, bf16[128,1024]{1,0:T(8,128)(2,1)S(1)}, u32[]{:S(2)}, u32[]{:S(2)}) %collective-permute-start.21) | collective-permute-done | bytes 262176 | tf_op jit(solution)/shard_map/cond/branch_2_fun/ppermute | solution.py:615
  62.2 0.1 collective-permute-start.22
  62.3 2.5 %down.28.refs_2_ = f32[128,2048]{1,0:T(8,128)S(1)} custom-call(bf16[128,1024]{1,0:T(8,128)(2,1)S(1)} %collective-permute-done.23.refs_0_, bf16[4096,2048]{1,0:T(8,128)(2,1)} %get-tuple-element.108.refs_0_.refs_1_, f32[128,2048]{1,0:T(8,128)S(1)} %down.27.refs_2_), custom_call_target="tpu_custom_call" | custom-call | flops 8388608 | bytes 65536 | tf_op jit(solution)/shard_map/cond/branch_2_fun/down/pallas_call | solution.py:489
  64.9 2.6 %down.29.before_ref = f32[128,2048]{1,0:T(8,128)S(1)} custom-call(bf16[128,1024]{1,0:T(8,128)(2,1)S(1)} %collective-permute-done.21.refs_0_, bf16[4096,2048]{1,0:T(8,128)(2,1)} %get-tuple-element.108.refs_0_.refs_1_, f32[128,2048]{1,0:T(8,128)S(1)} %down.28.refs_2_), custom_call_target="tpu_custom_call" | custom-call | flops 8388608 | bytes 65536 | tf_op jit(solution)/shard_map/cond/branch_2_fun/down/pallas_call | solution.py:489
  67.5 1.2 %collective-permute-done.22.a_ref = bf16[128,1024]{1,0:T(8,128)(2,1)S(1)} collective-permute-done((bf16[128,1024]{1,0:T(8,128)(2,1)S(1)}, bf16[128,1024]{1,0:T(8,128)(2,1)S(1)}, u32[]{:S(2)}, u32[]{:S(2)}) %collective-permute-start.22) | collective-permute-done | bytes 262176 | tf_op jit(solution)/shard_map/cond/branch_2_fun/ppermute | solution.py:615
  68.7 2.2 %down_unpack.9 = (bf16[384,512]{1,0:T(8,128)(2,1)S(1)}, bf16[384,512]{1,0:T(8,128)(2,1)S(1)}) custom-call(bf16[2,16,16,128]{3,2,1,0:T(8,128)(2,1)S(1)} %back_picks.9.picks_ref, bf16[128,1024]{1,0:T(8,128)(2,1)S(1)} %collective-permute-done.22.a_ref, bf16[1024,2048]{1,0:T(8,128)(2,1)S(1)} %get-tuple-element.113.w_ref, f32[128,2048]{1,0:T(8,128)S(1)} %down.29.before_ref), custom_call_target="tpu_custom_call" | custom-call | flops 8388608 | bytes 16384 | tf_op jit(solution)/shard_map/cond/branch_2_fun/down_unpack/pallas_call | solution.py:567
  71.2 0.1 collective-permute-start.64
  71.3 1.7 %collective-permute-done.64 = bf16[384,512]{1,0:T(8,128)(2,1)S(1)} collective-permute-done((bf16[384,512]{1,0:T(8,128)(2,1)S(1)}, bf16[384,512]{1,0:T(8,128)(2,1)S(1)}, u32[]{:S(2)}, u32[]{:S(2)}) %collective-permute-start.64) | collective-permute-done | bytes 393248 | tf_op jit(solution)/shard_map/ppermute | solution.py:615
  73.0 1.6 %collective-permute-start.67 = (bf16[96,512]{1,0:T(8,128)(2,1)S(1)}, bf16[96,512]{1,0:T(8,128)(2,1)S(1)}, u32[]{:S(2)}, u32[]{:S(2)}) collective-permute-start(bf16[96,512]{1,0:T(8,128)(2,1)S(1)} %add_convert_fusion.1), channel_id=1, source_target_pairs={{0,2},{1,3},{2,0},{3,1},{4,6},{5,7},{6,4},{7,5},{8,10},{9,11},{10,... | collective-permute-start | bytes 294920 | tf_op jit(solution)/shard_map/ppermute | solution.py:615
  74.6 3.3 %collective-permute-done.67 = bf16[96,512]{1,0:T(8,128)(2,1)S(1)} collective-permute-done((bf16[96,512]{1,0:T(8,128)(2,1)S(1)}, bf16[96,512]{1,0:T(8,128)(2,1)S(1)}, u32[]{:S(2)}, u32[]{:S(2)}) %collective-permute-start.67) | collective-permute-done | bytes 98336 | tf_op jit(solution)/shard_map/ppermute | solution.py:615
  77.9 0.1 add_convert_fusion
  78.0 1.6 %collective-permute-start.65 = (bf16[96,512]{1,0:T(8,128)(2,1)S(1)}, bf16[96,512]{1,0:T(8,128)(2,1)S(1)}, u32[]{:S(2)}, u32[]{:S(2)}) collective-permute-start(bf16[96,512]{1,0:T(8,128)(2,1)S(1)} %get-tuple-element.231), channel_id=1, source_target_pairs={{0,2},{1,3},{2,0},{3,1},{4,6},{5,7},{6,4},{7,5},{8,10},{9,11},{10,... | collective-permute-start | bytes 294920 | tf_op jit(solution)/shard_map/ppermute | solution.py:615
  79.6 4.6 %collective-permute-start.69 = (bf16[48,512]{1,0:T(8,128)(2,1)S(1)}, bf16[48,512]{1,0:T(8,128)(2,1)S(1)}, u32[]{:S(2)}, u32[]{:S(2)}) collective-permute-start(bf16[48,512]{1,0:T(8,128)(2,1)S(1)} %get-tuple-element.232), channel_id=1, source_target_pairs={{0,12},{4,8},{8,4},{12,0},{1,13},{5,9},{9,5},{13,1},{2,14},{6,10},... | collective-permute-start | bytes 147464 | tf_op jit(solution)/shard_map/ppermute | solution.py:615
  84.2 0.7 collective-permute-start.66
  84.9 1.4 %collective-permute-done.69.refs_9_ = bf16[48,512]{1,0:T(8,128)(2,1)S(1)} collective-permute-done((bf16[48,512]{1,0:T(8,128)(2,1)S(1)}, bf16[48,512]{1,0:T(8,128)(2,1)S(1)}, u32[]{:S(2)}, u32[]{:S(2)}) %collective-permute-start.69) | collective-permute-done | bytes 49184 | tf_op jit(solution)/shard_map/ppermute | solution.py:615
  86.4 2.8 %collective-permute-done.68.refs_8_ = bf16[48,512]{1,0:T(8,128)(2,1)S(1)} collective-permute-done((bf16[48,512]{1,0:T(8,128)(2,1)S(1)}, bf16[48,512]{1,0:T(8,128)(2,1)S(1)}, u32[]{:S(2)}, u32[]{:S(2)}) %collective-permute-start.68) | collective-permute-done | bytes 49184 | tf_op jit(solution)/shard_map/ppermute | solution.py:615
  89.2 1.0 %finish.1 = bf16[15,8192]{1,0:T(8,128)(2,1)} custom-call(bf16[4,16,48]{2,1,0:T(8,128)(2,1)S(1)} %get-tuple-element.191.picks_ref, f32[15,2048]{1,0:T(8,128)S(1)} %get-tuple-element.199.refs_0_, f32[15,2048]{1,0:T(8,128)S(1)} %get-tuple-element.200.refs_1_, f32[15,2048]{1,0:T(8,128)S(1)} %get-tuple-element.201.refs_2_, ...), custom_call_target="tpu_custom_call" | custom-call | flops 61440 | bytes 15360 | tf_op jit(solution)/shard_map/finish/pallas_call | solution.py:603
  (24 shorter events, 0.2 us)
Async XLA Ops:
  5.6 7.6 %collective-permute-start.56 = (bf16[48,1024]{1,0:T(8,128)(2,1)S(1)}, bf16[48,1024]{1,0:T(8,128)(2,1)S(1)}, u32[]{:S(2)}, u32[]{:S(2)}) collective-permute-start(bf16[48,1024]{1,0:T(8,128)(2,1)S(1)} %pad_maximum_fusion.7), channel_id=1, source_target_pairs={{0,8},{4,12},{8,0},{12,4},{1,9},{5,13},{9,1},{13,5},{2,10},{6,14},... | collective-permute-start | bytes 294920 | tf_op jit(solution)/shard_map/ppermute | solution.py:615
  13.2 4.7 %collective-permute-start.57 = (bf16[48,1024]{1,0:T(8,128)(2,1)S(1)}, bf16[48,1024]{1,0:T(8,128)(2,1)S(1)}, u32[]{:S(2)}, u32[]{:S(2)}) collective-permute-start(bf16[48,1024]{1,0:T(8,128)(2,1)S(1)} %pad_maximum_fusion.9), channel_id=1, source_target_pairs={{0,4},{4,0},{8,12},{12,8},{1,5},{5,1},{9,13},{13,9},{2,6},{6,2},{1... | collective-permute-start | bytes 294920 | tf_op jit(solution)/shard_map/ppermute | solution.py:615
  14.0 5.9 %collective-permute-start.60 = (bf16[48,1024]{1,0:T(8,128)(2,1)S(1)}, bf16[48,1024]{1,0:T(8,128)(2,1)S(1)}, u32[]{:S(2)}, u32[]{:S(2)}) collective-permute-start(bf16[48,1024]{1,0:T(8,128)(2,1)S(1)} %pad_maximum_fusion.8.refs_0_), channel_id=1, source_target_pairs={{0,2},{1,3},{2,0},{3,1},{4,6},{5,7},{6,4},{7,5},{8,10},{9,11},{10,... | collective-permute-start | bytes 294920 | tf_op jit(solution)/shard_map/ppermute | solution.py:615
  17.9 4.6 %collective-permute-start.61 = (bf16[48,1024]{1,0:T(8,128)(2,1)S(1)}, bf16[48,1024]{1,0:T(8,128)(2,1)S(1)}, u32[]{:S(2)}, u32[]{:S(2)}) collective-permute-start(bf16[48,1024]{1,0:T(8,128)(2,1)S(1)} %collective-permute-done.57.refs_1_), channel_id=1, source_target_pairs={{0,2},{1,3},{2,0},{3,1},{4,6},{5,7},{6,4},{7,5},{8,10},{9,11},{10,... | collective-permute-start | bytes 294920 | tf_op jit(solution)/shard_map/ppermute | solution.py:615
  19.4 3.1 %collective-permute-start.58 = (bf16[48,1024]{1,0:T(8,128)(2,1)S(1)}, bf16[48,1024]{1,0:T(8,128)(2,1)S(1)}, u32[]{:S(2)}, u32[]{:S(2)}) collective-permute-start(bf16[48,1024]{1,0:T(8,128)(2,1)S(1)} %pad_maximum_fusion.8.refs_0_), channel_id=1, source_target_pairs={{0,1},{1,0},{2,3},{3,2},{4,5},{5,4},{6,7},{7,6},{8,9},{9,8},{10,11... | collective-permute-start | bytes 294920 | tf_op jit(solution)/shard_map/ppermute | solution.py:615
  19.4 3.1 %collective-permute-start.59 = (bf16[48,1024]{1,0:T(8,128)(2,1)S(1)}, bf16[48,1024]{1,0:T(8,128)(2,1)S(1)}, u32[]{:S(2)}, u32[]{:S(2)}) collective-permute-start(bf16[48,1024]{1,0:T(8,128)(2,1)S(1)} %collective-permute-done.57.refs_1_), channel_id=1, source_target_pairs={{0,1},{1,0},{2,3},{3,2},{4,5},{5,4},{6,7},{7,6},{8,9},{9,8},{10,11... | collective-permute-start | bytes 294920 | tf_op jit(solution)/shard_map/ppermute | solution.py:615
  19.9 2.6 %collective-permute-start.62 = (bf16[48,1024]{1,0:T(8,128)(2,1)S(1)}, bf16[48,1024]{1,0:T(8,128)(2,1)S(1)}, u32[]{:S(2)}, u32[]{:S(2)}) collective-permute-start(bf16[48,1024]{1,0:T(8,128)(2,1)S(1)} %collective-permute-done.60.refs_4_), channel_id=1, source_target_pairs={{0,1},{1,0},{2,3},{3,2},{4,5},{5,4},{6,7},{7,6},{8,9},{9,8},{10,11... | collective-permute-start | bytes 294920 | tf_op jit(solution)/shard_map/ppermute | solution.py:615
  22.5 1.3 %collective-permute-start.63 = (bf16[48,1024]{1,0:T(8,128)(2,1)S(1)}, bf16[48,1024]{1,0:T(8,128)(2,1)S(1)}, u32[]{:S(2)}, u32[]{:S(2)}) collective-permute-start(bf16[48,1024]{1,0:T(8,128)(2,1)S(1)} %collective-permute-done.61.refs_5_), channel_id=1, source_target_pairs={{0,1},{1,0},{2,3},{3,2},{4,5},{5,4},{6,7},{7,6},{8,9},{9,8},{10,11... | collective-permute-start | bytes 294920 | tf_op jit(solution)/shard_map/ppermute | solution.py:615
  27.4 5.6 %collective-permute-start.17 = (bf16[128,512]{1,0:T(8,128)(2,1)S(1)}, bf16[128,512]{1,0:T(8,128)(2,1)S(1)}, u32[]{:S(2)}, u32[]{:S(2)}) collective-permute-start(bf16[128,512]{1,0:T(8,128)(2,1)S(1)} %slice.157), channel_id=1, source_target_pairs={{0,4},{4,0},{8,12},{12,8},{1,5},{5,1},{9,13},{13,9},{2,6},{6,2},{1... | collective-permute-start | bytes 393224 | tf_op jit(solution)/shard_map/cond/branch_2_fun/ppermute | solution.py:615
  31.6 8.2 %collective-permute-start.16 = (bf16[128,512]{1,0:T(8,128)(2,1)S(1)}, bf16[128,512]{1,0:T(8,128)(2,1)S(1)}, u32[]{:S(2)}, u32[]{:S(2)}) collective-permute-start(bf16[128,512]{1,0:T(8,128)(2,1)S(1)} %slice_bitcast_fusion.7), channel_id=1, source_target_pairs={{0,4},{4,0},{8,12},{12,8},{1,5},{5,1},{9,13},{13,9},{2,6},{6,2},{1... | collective-permute-start | bytes 393224 | tf_op jit(solution)/shard_map/cond/branch_2_fun/ppermute | solution.py:615
  33.1 12.0 %collective-permute-start.19 = (bf16[128,512]{1,0:T(8,128)(2,1)S(1)}, bf16[128,512]{1,0:T(8,128)(2,1)S(1)}, u32[]{:S(2)}, u32[]{:S(2)}) collective-permute-start(bf16[128,512]{1,0:T(8,128)(2,1)S(1)} %fusion.16), channel_id=1, source_target_pairs={{0,8},{4,12},{8,0},{12,4},{1,9},{5,13},{9,1},{13,5},{2,10},{6,14},... | collective-permute-start | bytes 393224 | tf_op jit(solution)/shard_map/cond/branch_2_fun/ppermute | solution.py:615
  39.7 8.8 %collective-permute-start.18 = (bf16[2,128,512]{2,1,0:T(8,128)(2,1)S(1)}, bf16[2,128,512]{2,1,0:T(8,128)(2,1)S(1)}, u32[]{:S(2)}, u32[]{:S(2)}) collective-permute-start(bf16[2,128,512]{2,1,0:T(8,128)(2,1)S(1)} %up.28), channel_id=1, source_target_pairs={{0,4},{4,0},{8,12},{12,8},{1,5},{5,1},{9,13},{13,9},{2,6},{6,2},{1... | collective-permute-start | bytes 786440 | tf_op jit(solution)/shard_map/cond/branch_2_fun/ppermute | solution.py:615
  40.0 7.6 %collective-permute-start.20 = (bf16[128,512]{1,0:T(8,128)(2,1)S(1)}, bf16[128,512]{1,0:T(8,128)(2,1)S(1)}, u32[]{:S(2)}, u32[]{:S(2)}) collective-permute-start(bf16[128,512]{1,0:T(8,128)(2,1)S(1)} %fusion.17), channel_id=1, source_target_pairs={{0,8},{4,12},{8,0},{12,4},{1,9},{5,13},{9,1},{13,5},{2,10},{6,14},... | collective-permute-start | bytes 393224 | tf_op jit(solution)/shard_map/cond/branch_2_fun/ppermute | solution.py:615
  48.6 13.6 %collective-permute-start.21 = (bf16[128,1024]{1,0:T(8,128)(2,1)S(1)}, bf16[128,1024]{1,0:T(8,128)(2,1)S(1)}, u32[]{:S(2)}, u32[]{:S(2)}) collective-permute-start(bf16[128,1024]{1,0:T(8,128)(2,1)S(1)} %pad_maximum_fusion.2.refs_0_), channel_id=1, source_target_pairs={{0,8},{4,12},{8,0},{12,4},{1,9},{5,13},{9,1},{13,5},{2,10},{6,14},... | collective-permute-start | bytes 786440 | tf_op jit(solution)/shard_map/cond/branch_2_fun/ppermute | solution.py:615
  51.3 11.1 %collective-permute-start.23 = (bf16[128,1024]{1,0:T(8,128)(2,1)S(1)}, bf16[128,1024]{1,0:T(8,128)(2,1)S(1)}, u32[]{:S(2)}, u32[]{:S(2)}) collective-permute-start(bf16[128,1024]{1,0:T(8,128)(2,1)S(1)} %pad_maximum_fusion.2.refs_0_), channel_id=1, source_target_pairs={{0,4},{4,0},{8,12},{12,8},{1,5},{5,1},{9,13},{13,9},{2,6},{6,2},{1... | collective-permute-start | bytes 786440 | tf_op jit(solution)/shard_map/cond/branch_2_fun/ppermute | solution.py:615
  62.2 6.5 %collective-permute-start.22 = (bf16[128,1024]{1,0:T(8,128)(2,1)S(1)}, bf16[128,1024]{1,0:T(8,128)(2,1)S(1)}, u32[]{:S(2)}, u32[]{:S(2)}) collective-permute-start(bf16[128,1024]{1,0:T(8,128)(2,1)S(1)} %collective-permute-done.21.refs_0_), channel_id=1, source_target_pairs={{0,4},{4,0},{8,12},{12,8},{1,5},{5,1},{9,13},{13,9},{2,6},{6,2},{1... | collective-permute-start | bytes 786440 | tf_op jit(solution)/shard_map/cond/branch_2_fun/ppermute | solution.py:615
  71.2 1.8 %collective-permute-start.64 = (bf16[384,512]{1,0:T(8,128)(2,1)S(1)}, bf16[384,512]{1,0:T(8,128)(2,1)S(1)}, u32[]{:S(2)}, u32[]{:S(2)}) collective-permute-start(bf16[384,512]{1,0:T(8,128)(2,1)S(1)} %get-tuple-element.215), channel_id=1, source_target_pairs={{0,1},{1,0},{2,3},{3,2},{4,5},{5,4},{6,7},{7,6},{8,9},{9,8},{10,11... | collective-permute-start | bytes 1179656 | tf_op jit(solution)/shard_map/ppermute | solution.py:615
  73.0 4.9 %collective-permute-start.67 = (bf16[96,512]{1,0:T(8,128)(2,1)S(1)}, bf16[96,512]{1,0:T(8,128)(2,1)S(1)}, u32[]{:S(2)}, u32[]{:S(2)}) collective-permute-start(bf16[96,512]{1,0:T(8,128)(2,1)S(1)} %add_convert_fusion.1), channel_id=1, source_target_pairs={{0,2},{1,3},{2,0},{3,1},{4,6},{5,7},{6,4},{7,5},{8,10},{9,11},{10,... | collective-permute-start | bytes 294920 | tf_op jit(solution)/shard_map/ppermute | solution.py:615
  78.0 6.2 %collective-permute-start.65 = (bf16[96,512]{1,0:T(8,128)(2,1)S(1)}, bf16[96,512]{1,0:T(8,128)(2,1)S(1)}, u32[]{:S(2)}, u32[]{:S(2)}) collective-permute-start(bf16[96,512]{1,0:T(8,128)(2,1)S(1)} %get-tuple-element.231), channel_id=1, source_target_pairs={{0,2},{1,3},{2,0},{3,1},{4,6},{5,7},{6,4},{7,5},{8,10},{9,11},{10,... | collective-permute-start | bytes 294920 | tf_op jit(solution)/shard_map/ppermute | solution.py:615
  79.6 6.8 %collective-permute-start.69 = (bf16[48,512]{1,0:T(8,128)(2,1)S(1)}, bf16[48,512]{1,0:T(8,128)(2,1)S(1)}, u32[]{:S(2)}, u32[]{:S(2)}) collective-permute-start(bf16[48,512]{1,0:T(8,128)(2,1)S(1)} %get-tuple-element.232), channel_id=1, source_target_pairs={{0,12},{4,8},{8,4},{12,0},{1,13},{5,9},{9,5},{13,1},{2,14},{6,10},... | collective-permute-start | bytes 147464 | tf_op jit(solution)/shard_map/ppermute | solution.py:615
  84.2 5.0 %collective-permute-start.68 = (bf16[48,512]{1,0:T(8,128)(2,1)S(1)}, bf16[48,512]{1,0:T(8,128)(2,1)S(1)}, u32[]{:S(2)}, u32[]{:S(2)}) collective-permute-start(bf16[48,512]{1,0:T(8,128)(2,1)S(1)} %get-tuple-element.233), channel_id=1, source_target_pairs={{0,8},{4,12},{8,0},{12,4},{1,9},{5,13},{9,1},{13,5},{2,10},{6,14},... | collective-permute-start | bytes 147464 | tf_op jit(solution)/shard_map/ppermute | solution.py:615
  84.2 4.9 %collective-permute-start.66 = (bf16[48,512]{1,0:T(8,128)(2,1)S(1)}, bf16[48,512]{1,0:T(8,128)(2,1)S(1)}, u32[]{:S(2)}, u32[]{:S(2)}) collective-permute-start(bf16[48,512]{1,0:T(8,128)(2,1)S(1)} %get-tuple-element.234), channel_id=1, source_target_pairs={{0,4},{4,0},{8,12},{12,8},{1,5},{5,1},{9,13},{13,9},{2,6},{6,2},{1... | collective-permute-start | bytes 147464 | tf_op jit(solution)/shard_map/ppermute | solution.py:615
